TPU v7x, 32 devices: a whole 2x2x4 slice. The times are simulated.
32 devices in a mesh: groups: 2 (over x), blk: 16 (over z, y, core).
Axes of the slice: x: 2, y: 2, z: 4, core: 2. Of those that a mesh axis runs over, the one named last changes fastest.
Arguments:
- tokens: bfloat16 [8192, 8192], P(('groups', 'blk')), parts along dimension 0, may hold values from -6 to 6
- shrink_panels: bfloat16 [32, 8192, 64], P(None, 'blk'), may hold values from -0.0625 to 0.0625
- expand_panels: bfloat16 [32, 64, 8192], P(None, None, 'blk'), may hold values from -0.75 to 0.75
- adapter_scale: float32 [32], replicated, may hold values from 0.5 to 2
- block_adapter: int32 [128, 1], P('groups'), parts along dimension 0, may hold values from 0 to 31
- shard_counts: int32 [32], P('groups'), parts along dimension 0, may hold values from 1 to 256, as said below
Outputs:
- update: bfloat16 [8192, 8192], P(('groups', 'blk')), parts along dimension 0
There are 2 independent parts, one for each index of `groups`. A program takes and returns all parts, laid end to end along the dimension named above; an argument that names none is the same for every part. Nothing has to cross between parts.
Inputs may be any that keep to these rules, and one draw needn't show every extreme that they name: `shard_counts`: every shard holds at least one live row; in every draw some shard is full.
All inputs are finite; a program needn't handle non-finite values.
Results may differ from a plain program's by a relative error of at most 0.0049.
Values may be sent and summed in bfloat16 or wider, within the bound.
No kernel may reach another device: no remote copies, remote signals or barrier semaphores. Data moves between devices by JAX's collectives and lax.ppermute only.
A program may use at most 128 MiB of HBM per device.

v0:
```python
import jax
import jax.numpy as jnp
from jax import lax
from jax.sharding import PartitionSpec as P

BLOCK = 64


def body(tokens, shrink_panels, expand_panels, adapter_scale, block_adapter, shard_counts):
    shard_rows, model_width = tokens.shape
    adapter_ids = block_adapter[:, 0]
    own_blocks = shard_rows // BLOCK
    shrink_sel = jnp.take(shrink_panels, adapter_ids, axis=0)
    expand_sel = jnp.take(expand_panels, adapter_ids, axis=0)
    blocked = tokens.reshape(own_blocks, BLOCK, model_width)
    down_maps = lax.all_to_all(shrink_sel, "blk", split_axis=0, concat_axis=1, tiled=True)
    up_maps = lax.all_to_all(expand_sel, "blk", split_axis=0, concat_axis=2, tiled=True)
    shard_index = lax.axis_index("blk")
    mine = lax.dynamic_slice_in_dim(adapter_ids, shard_index * own_blocks, own_blocks, 0)
    scales = jnp.take(adapter_scale, mine, axis=0)
    shrunk = jnp.einsum(
        "bkc,bcr->bkr", blocked, down_maps, preferred_element_type=jnp.float32
    ).astype(jnp.bfloat16)
    expanded = jnp.einsum("bkr,brc->bkc", shrunk, up_maps, preferred_element_type=jnp.float32)
    expanded = expanded * scales[:, None, None]
    own_count = lax.dynamic_index_in_dim(shard_counts, shard_index, 0, keepdims=False)
    within = lax.iota(jnp.int32, shard_rows)
    live_rows = (within < own_count).reshape(own_blocks, BLOCK, 1)
    masked_out = jnp.where(live_rows, expanded, 0.0).astype(jnp.bfloat16)
    return masked_out.reshape(shard_rows, model_width)


def solution(mesh):
    return jax.shard_map(
        body,
        mesh=mesh,
        in_specs=(
            P(("groups", "blk"), None),
            P(None, "blk", None),
            P(None, None, "blk"),
            P(),
            P("groups", None),
            P("groups"),
        ),
        out_specs=P(("groups", "blk"), None),
        check_vma=False,
    )
```

profile of v0, /device:TPU:13, one launch (start us, length us, event | category | flops | bytes accessed | tf_op | source)
XLA Modules:
  0.0 228.5 jit_solution(18072058476179573344)
XLA Ops:
  0.0 0.0 copy-start
  0.0 0.8 and_bitcast_fusion
  0.8 0.7 fusion.2
  1.5 0.1 copy-done
  1.6 2.8 %gather_fusion.1 = bf16[64,64,512]{2,1,0:T(8,128)(2,1)} fusion(bf16[32,64,512]{2,1,0:T(8,128)(2,1)S(1)} %copy-done, s32[1024]{0:T(1024)S(1)} %pad_clamp_fusion.1), kind=kCustom, calls=%fused_computation.1 | custom fusion | bytes 8388864 | tf_op jit(solution)/shard_map/jit(_take)/gather | solution.py:14
  4.4 4.6 %broadcast_select_fusion = bf16[64,64,512]{2,1,0:T(8,128)(2,1)} fusion(bf16[64,64,512]{2,1,0:T(8,128)(2,1)} %gather_fusion.1, pred[64]{0:T(512)(128)(4,1)S(1)} %and_bitcast_fusion), kind=kLoop, calls=%fused_computation.8 | loop fusion | flops 2097152 | bytes 8388672 | tf_op jit(solution)/shard_map/jit(_take)/select_n | solution.py:14
  9.1 6.6 %all-to-all-start.1 = ((bf16[64,64,512]{2,1,0:T(8,128)(2,1)}), bf16[64,64,512]{2,1,0:T(8,128)(2,1)}, u32[]{:S(2)}, u32[]{:S(2)}) async-start(bf16[64,64,512]{2,1,0:T(8,128)(2,1)} %broadcast_select_fusion), calls=%async_computation.1 | async-start | bytes 8388608 | tf_op jit(solution)/shard_map/all_to_all | solution.py:17
  15.6 4.4 %gather_fusion = bf16[64,512,64]{1,2,0:T(8,128)(2,1)} fusion(bf16[32,512,64]{1,2,0:T(8,128)(2,1)} %param.7, s32[1024]{0:T(1024)S(1)} %pad_clamp_fusion.1), kind=kCustom, calls=%fused_computation | custom fusion | bytes 8388864 | tf_op jit(solution)/shard_map/jit(_take)/gather | solution.py:13
  20.0 4.6 %broadcast_select_fusion.1 = bf16[64,512,64]{1,2,0:T(8,128)(2,1)} fusion(bf16[64,512,64]{1,2,0:T(8,128)(2,1)} %gather_fusion, pred[64]{0:T(512)(128)(4,1)S(1)} %and_bitcast_fusion), kind=kLoop, calls=%fused_computation.9 | loop fusion | flops 2097152 | bytes 8388672 | tf_op jit(solution)/shard_map/jit(_take)/select_n | solution.py:13
  24.6 83.5 %all-to-all-done.1 = bf16[64,64,512]{2,1,0:T(8,128)(2,1)} async-done(((bf16[64,64,512]{2,1,0:T(8,128)(2,1)}), bf16[64,64,512]{2,1,0:T(8,128)(2,1)}, u32[]{:S(2)}, u32[]{:S(2)}) %all-to-all-start.1) | async-done | bytes 4194336 | tf_op jit(solution)/shard_map/all_to_all | solution.py:17
  108.1 4.9 %all-to-all-start = ((bf16[64,512,64]{1,2,0:T(8,128)(2,1)}), bf16[64,512,64]{1,2,0:T(8,128)(2,1)}, u32[]{:S(2)}, u32[]{:S(2)}) async-start(bf16[64,512,64]{1,2,0:T(8,128)(2,1)} %broadcast_select_fusion.1), calls=%async_computation | async-start | bytes 8388608 | tf_op jit(solution)/shard_map/all_to_all | solution.py:16
  113.0 0.0 copy-done.3
  113.0 0.6 dynamic_slice.7
  113.6 0.0 copy-done.2
  113.6 0.1 fusion.3
  113.7 0.6 gather_fusion.2
  114.3 0.7 add_compare_fusion
  115.0 0.1 bitcast_select_fusion
  115.1 6.6 %copy.12 = bf16[16,4,64,512]{3,0,2,1:T(8,128)(2,1)} copy(bf16[16,4,64,512]{3,2,1,0:T(8,128)(2,1)} %bitcast.6) | data formatting | bytes 8388608 | tf_op jit(solution)/shard_map/all_to_all | solution.py:17
  121.7 7.4 %all_to_all.33 = bf16[4,64,8192]{2,1,0:T(8,128)(2,1)} reshape(bf16[4,64,16,512]{3,2,1,0:T(8,128)(2,1)} %bitcast.28) | data formatting | bytes 8388608 | tf_op jit(solution)/shard_map/all_to_all | solution.py:17
  129.0 76.4 %all-to-all-done = bf16[64,512,64]{1,2,0:T(8,128)(2,1)} async-done(((bf16[64,512,64]{1,2,0:T(8,128)(2,1)}), bf16[64,512,64]{1,2,0:T(8,128)(2,1)}, u32[]{:S(2)}, u32[]{:S(2)}) %all-to-all-start) | async-done | bytes 4194336 | tf_op jit(solution)/shard_map/all_to_all | solution.py:16
  205.5 6.6 %copy.13 = bf16[16,4,512,64]{2,0,3,1:T(8,128)(2,1)} copy(bf16[16,4,512,64]{2,3,1,0:T(8,128)(2,1)} %bitcast.3) | data formatting | bytes 8388608 | tf_op jit(solution)/shard_map/all_to_all | solution.py:16
  212.1 7.4 %all_to_all.29 = bf16[4,8192,64]{1,2,0:T(8,128)(2,1)} reshape(bf16[4,16,512,64]{2,1,3,0:T(8,128)(2,1)} %bitcast.29) | data formatting | bytes 8388608 | tf_op jit(solution)/shard_map/all_to_all | solution.py:16
  219.5 9.0 %fusion.1 = bf16[4,64,8192]{2,1,0:T(8,128)(2,1)} fusion(bf16[4,64,8192]{2,1,0:T(8,128)(2,1)} %all_to_all.33, f32[4]{0:T(128)S(1)} %bitcast_select_fusion, pred[4,64]{1,0:T(4,128)(4,1)S(1)} %add_compare_fusion, bf16[4,8192,64]{1,2,0:T(8,128)(2,1)} %all_to_all.29, bf16[4,64,8192]{2,1,0:T(8,128)(2,1)} %bitcast.30), kind=kOutput, calls=%fused_computation.5 | convolution fusion | flops 543178752 | bytes 16777488 | tf_op jit(solution)/shard_map/bkr,brc->bkc/dot_general | solution.py:24
  (6 shorter events, 0.0 us)
Async XLA Ops:
  0.0 1.6 copy-start
  9.1 99.0 %all-to-all-start.1 = ((bf16[64,64,512]{2,1,0:T(8,128)(2,1)}), bf16[64,64,512]{2,1,0:T(8,128)(2,1)}, u32[]{:S(2)}, u32[]{:S(2)}) async-start(bf16[64,64,512]{2,1,0:T(8,128)(2,1)} %broadcast_select_fusion), calls=%async_computation.1 | async-start | bytes 8388608 | tf_op jit(solution)/shard_map/all_to_all | solution.py:17
  24.6 88.4 %copy-start.3 = (s32[16]{0:T(128)S(1)}, s32[16]{0:T(128)}, u32[]{:S(2)}) copy-start(s32[16]{0:T(128)} %param.11) | copy-start | bytes 196
  24.6 89.0 %copy-start.2 = (s32[64,1]{0,1:T(1,128)S(1)}, s32[64,1]{0,1:T(1,128)}, u32[]{:S(2)}) copy-start(s32[64,1]{0,1:T(1,128)} %param.10) | copy-start | bytes 772
  24.6 89.1 %copy-start.1 = (f32[32]{0:T(128)S(1)}, f32[32]{0:T(128)}, u32[]{:S(2)}) copy-start(f32[32]{0:T(128)} %param.9) | copy-start | bytes 388
  108.1 97.4 %all-to-all-start = ((bf16[64,512,64]{1,2,0:T(8,128)(2,1)}), bf16[64,512,64]{1,2,0:T(8,128)(2,1)}, u32[]{:S(2)}, u32[]{:S(2)}) async-start(bf16[64,512,64]{1,2,0:T(8,128)(2,1)} %broadcast_select_fusion.1), calls=%async_computation | async-start | bytes 8388608 | tf_op jit(solution)/shard_map/all_to_all | solution.py:16
where the time goes:
time: 229 us; the launch traced here: 228 us
  waiting for transfers between devices  160 us (70%)
  local copies, waits for them, and re-layouts  36.5 us (16%)
  other arithmetic  11.5 us (5%)
  starting transfers between devices  11.5 us (5%)
  matrix products  9 us (4%)
    all_to_all x1, waiting for transfers between devices, body(): lax.all_to_all(expand_sel, 'blk', split_axis=0, concat_axis=2, tiled=True)  83.5 us
    all_to_all x1, waiting for transfers between devices, body(): lax.all_to_all(shrink_sel, 'blk', split_axis=0, concat_axis=1, tiled=True)  76.4 us
    all_to_all x2, local copies, waits for them, and re-layouts, body(): lax.all_to_all(shrink_sel, 'blk', split_axis=0, concat_axis=1, tiled=True)  14 us
    all_to_all x2, local copies, waits for them, and re-layouts, body(): lax.all_to_all(expand_sel, 'blk', split_axis=0, concat_axis=2, tiled=True)  14 us
    dot_general x1, matrix products, body(): jnp.einsum('bkr,brc->bkc', shrunk, up_maps, preferred_element_type=jnp.fl...  9 us
    all_to_all x1, starting transfers between devices, body(): lax.all_to_all(expand_sel, 'blk', split_axis=0, concat_axis=2, tiled=True)  6.55 us
    select_n x2, other arithmetic, body(): shrink_sel = jnp.take(shrink_panels, adapter_ids, axis=0)  5.25 us
    all_to_all x1, starting transfers between devices, body(): lax.all_to_all(shrink_sel, 'blk', split_axis=0, concat_axis=1, tiled=True)  4.91 us
  transfers between devices with their start and end apart: 2, of which 2 were waited for; matrix products, arithmetic and copies ran while one was open for 8% of the time, Pallas kernels for 0%

commit v1 on v0

v1 whole, which is shorter than its diff:
```python
import functools

import jax
import jax.numpy as jnp
from jax import lax
from jax.experimental import pallas as pl
from jax.experimental.pallas import tpu as pltpu
from jax.sharding import PartitionSpec as P

BLOCK = 64


def pack_kernel(ids, panels, out, sem):
    for i in range(out.shape[0]):
        pltpu.make_async_copy(panels.at[ids[i]], out.at[i], sem).start()
    pltpu.make_async_copy(out, out, sem).wait()


def pack(ids, panels):
    count = ids.shape[0]
    return pl.pallas_call(
        pack_kernel,
        out_shape=jax.ShapeDtypeStruct((count, *panels.shape[1:]), panels.dtype),
        in_specs=[pl.BlockSpec(memory_space=pltpu.SMEM), pl.BlockSpec(memory_space=pl.ANY)],
        out_specs=pl.BlockSpec(memory_space=pl.ANY),
        scratch_shapes=[pltpu.SemaphoreType.DMA],
        cost_estimate=pl.CostEstimate(
            flops=0, bytes_accessed=2 * count * panels[0].size * panels.dtype.itemsize, transcendentals=0
        ),
        name="pack",
    )(ids, panels)


def shrink_kernel(tokens, maps, out):
    total = jnp.zeros(out.shape, jnp.float32)
    width = maps.shape[-1]
    for source in range(maps.shape[0]):
        total += lax.dot_general(
            tokens[:, source * width : (source + 1) * width],
            maps[source, 0],
            (((1,), (1,)), ((), ())),
            preferred_element_type=jnp.float32,
        )
    out[...] = total.astype(out.dtype)


def shrink(tokens, maps):
    sources, own, rank, width = maps.shape
    return pl.pallas_call(
        shrink_kernel,
        grid=(own,),
        out_shape=jax.ShapeDtypeStruct((own * BLOCK, rank), tokens.dtype),
        in_specs=[
            pl.BlockSpec((BLOCK, tokens.shape[1]), lambda b: (b, 0)),
            pl.BlockSpec((sources, 1, rank, width), lambda b: (0, b, 0, 0)),
        ],
        out_specs=pl.BlockSpec((BLOCK, rank), lambda b: (b, 0)),
        compiler_params=pltpu.CompilerParams(vmem_limit_bytes=32 * 2**20),
        cost_estimate=pl.CostEstimate(
            flops=2 * tokens.size * rank, bytes_accessed=2 * (tokens.size + maps.size), transcendentals=0
        ),
        name="shrink",
    )(tokens, maps)


def expand_kernel(ids, count, scales, shrunk, maps, out):
    b = pl.program_id(0)
    scale = scales[ids[b]]
    width = maps.shape[-1]
    rows = b * BLOCK + lax.broadcasted_iota(jnp.int32, (BLOCK, width), 0)
    live = rows < count[0]
    for source in range(maps.shape[0]):
        part = jnp.dot(shrunk[...], maps[source, 0], preferred_element_type=jnp.float32)
        out[:, source * width : (source + 1) * width] = jnp.where(live, part * scale, 0.0).astype(out.dtype)


def expand(ids, count, scales, shrunk, maps):
    sources, own, rank, width = maps.shape
    smem = pl.BlockSpec(memory_space=pltpu.SMEM)
    return pl.pallas_call(
        expand_kernel,
        grid=(own,),
        out_shape=jax.ShapeDtypeStruct((own * BLOCK, sources * width), maps.dtype),
        in_specs=[
            smem,
            smem,
            smem,
            pl.BlockSpec((BLOCK, rank), lambda b: (b, 0)),
            pl.BlockSpec((sources, 1, rank, width), lambda b: (0, b, 0, 0)),
        ],
        out_specs=pl.BlockSpec((BLOCK, sources * width), lambda b: (b, 0)),
        compiler_params=pltpu.CompilerParams(vmem_limit_bytes=32 * 2**20),
        cost_estimate=pl.CostEstimate(
            flops=2 * maps.size * BLOCK, bytes_accessed=4 * maps.size, transcendentals=0
        ),
        name="expand",
    )(ids, count, scales, shrunk, maps)


def body(tokens, shrink_panels, expand_panels, adapter_scale, block_adapter, shard_counts):
    devices = shard_counts.shape[0]
    own = tokens.shape[0] // BLOCK
    ids = block_adapter.reshape(-1)
    me = lax.axis_index("blk")
    mine = lax.dynamic_slice_in_dim(ids, me * own, own, 0)
    count = lax.dynamic_slice_in_dim(shard_counts, me, 1, 0)

    def exchange(panels):
        sent = pack(ids, panels)
        got = lax.all_to_all(sent, "blk", split_axis=0, concat_axis=0, tiled=True)
        return got.reshape(devices, own, *panels.shape[1:])

    down = exchange(jnp.swapaxes(shrink_panels, 1, 2))
    up = exchange(expand_panels)
    shrunk = shrink(tokens, down)
    return expand(mine, count, adapter_scale, shrunk, up)


def solution(mesh):
    return jax.shard_map(
        body,
        mesh=mesh,
        in_specs=(
            P(("groups", "blk"), None),
            P(None, "blk", None),
            P(None, None, "blk"),
            P(),
            P("groups", None),
            P("groups"),
        ),
        out_specs=P(("groups", "blk"), None),
        check_vma=False,
    )
```

time: 229 us -> 369 us (1.61)
  Pallas kernels: 0 us -> 268 us
  waiting for transfers between devices: 160 us -> 85.7 us
  local copies, waits for them, and re-layouts: 36.5 us -> 2.89 us
  other arithmetic: 11.5 us -> 0 us
  matrix products: 9 us -> 0 us
    pallas_call x0 -> x4, Pallas kernels: none -> 268 us  [the longest x2 258 us: pack(): pl.pallas_call(pack_kernel, out_shape=jax.ShapeDtypeStruct((count, *panel...]
    all_to_all x2, waiting for transfers between devices: 160 us -> 85.7 us  [exchange(): got = lax.all_to_all(sent, 'blk', split_axis=0, concat_axis=0, tiled=True)]
    all_to_all x4 -> x0, local copies, waits for them, and re-layouts: 28 us -> none  [the longest x2 14 us: body(): lax.all_to_all(shrink_sel, 'blk', split_axis=0, concat_axis=1, tiled=True)]
    select_n x5 -> x0, other arithmetic: 10 us -> none  [the longest x2 5.25 us: body(): shrink_sel = jnp.take(shrink_panels, adapter_ids, axis=0)]
    dot_general x1 -> x0, matrix products: 9 us -> none  [body(): jnp.einsum('bkr,brc->bkc', shrunk, up_maps, preferred_element_type=jnp.fl...]
    gather x3 -> x0, local copies, waits for them, and re-layouts: 7.83 us -> none  [the longest x1 4.37 us: body(): shrink_sel = jnp.take(shrink_panels, adapter_ids, axis=0)]
  transfers between devices with their start and end apart: 2 -> 2, of which waited for: 2 -> 1; matrix products, arithmetic and copies ran while one was open for 8% -> 0% of each run, Pallas kernels for 0% -> 36%
where the time goes in v1:
time: 369 us
  Pallas kernels  268 us (73%)
  waiting for transfers between devices  85.7 us (23%)
  starting transfers between devices  12.6 us (3%)
    pallas_call x2, Pallas kernels, pack(): pl.pallas_call(pack_kernel, out_shape=jax.ShapeDtypeStruct((count, *panel...  258 us
    all_to_all x2, waiting for transfers between devices, exchange(): got = lax.all_to_all(sent, 'blk', split_axis=0, concat_axis=0, tiled=True)  85.7 us
    all_to_all x2, starting transfers between devices, exchange(): got = lax.all_to_all(sent, 'blk', split_axis=0, concat_axis=0, tiled=True)  12.6 us
  transfers between devices with their start and end apart: 2, of which 1 were waited for; matrix products, arithmetic and copies ran while one was open for 0% of the time, Pallas kernels for 36%

profile of v1, /device:TPU:13, one launch (start us, length us, event | category | flops | bytes accessed | tf_op | source)
XLA Modules:
  0.0 368.9 jit_solution(5538012304108107186)
XLA Ops:
  0.0 128.8 %pack.2 = bf16[64,64,512]{2,1,0:T(8,128)(2,1)} custom-call(s32[64]{0:T(128)} %bitcast.7, bf16[32,64,512]{2,1,0:T(8,128)(2,1)} %bitcast.6), custom_call_target="tpu_custom_call" | custom-call | bytes 8388608 | tf_op jit(solution)/shard_map/pack/pallas_call | solution.py:21
  128.8 6.6 %all-to-all-start = ((bf16[64,64,512]{2,1,0:T(8,128)(2,1)}), bf16[64,64,512]{2,1,0:T(8,128)(2,1)}, u32[]{:S(2)}, u32[]{:S(2)}) async-start(bf16[64,64,512]{2,1,0:T(8,128)(2,1)} %pack.2), calls=%async_computation | async-start | bytes 8388608 | tf_op jit(solution)/shard_map/all_to_all | solution.py:110
  135.4 128.8 %pack.3 = bf16[64,64,512]{2,1,0:T(8,128)(2,1)} custom-call(s32[64]{0:T(128)} %bitcast.8, bf16[32,64,512]{2,1,0:T(8,128)(2,1)} %panels.1), custom_call_target="tpu_custom_call" | custom-call | bytes 8388608 | tf_op jit(solution)/shard_map/pack/pallas_call | solution.py:21
  264.2 0.0 copy-start.3
  264.3 0.0 copy-start.2
  264.3 0.0 all-to-all-done
  264.3 6.0 %all-to-all-start.1 = ((bf16[64,64,512]{2,1,0:T(8,128)(2,1)}), bf16[64,64,512]{2,1,0:T(8,128)(2,1)}, u32[]{:S(2)}, u32[]{:S(2)}) async-start(bf16[64,64,512]{2,1,0:T(8,128)(2,1)} %pack.3), calls=%async_computation.1 | async-start | bytes 8388608 | tf_op jit(solution)/shard_map/all_to_all | solution.py:110
  270.3 0.0 copy-done.3
  270.3 0.6 dynamic_slice.10.count
  270.9 0.0 copy-done.2
  270.9 0.1 dynamic-slice_bitcast_fusion.ids
  271.0 0.0 copy-start
  271.0 2.2 copy-done
  273.2 0.0 copy-start.1
  273.2 3.8 %shrink.1.shrunk = bf16[256,64]{1,0:T(8,128)(2,1)S(1)} custom-call(bf16[256,8192]{1,0:T(8,128)(2,1)S(1)} %copy-done, bf16[16,4,64,512]{3,2,1,0:T(8,128)(2,1)} %bitcast.3.maps), custom_call_target="tpu_custom_call" | custom-call | flops 268435456 | bytes 8388608 | tf_op jit(solution)/shard_map/shrink/pallas_call | solution.py:49
  277.0 85.7 %all-to-all-done.1 = bf16[64,64,512]{2,1,0:T(8,128)(2,1)} async-done(((bf16[64,64,512]{2,1,0:T(8,128)(2,1)}), bf16[64,64,512]{2,1,0:T(8,128)(2,1)}, u32[]{:S(2)}, u32[]{:S(2)}) %all-to-all-start.1) | async-done | bytes 4194336 | tf_op jit(solution)/shard_map/all_to_all | solution.py:110
  362.8 0.0 copy-done.1
  362.8 6.2 %expand.1 = bf16[256,8192]{1,0:T(8,128)(2,1)} custom-call(s32[4]{0:T(128)S(1)} %dynamic-slice_bitcast_fusion.ids, s32[1]{0:T(128)} %dynamic_slice.10.count, f32[32]{0:T(128)S(1)} %copy-done.1, bf16[256,64]{1,0:T(8,128)(2,1)S(1)} %shrink.1.shrunk, bf16[16,4,64,512]{3,2,1,0:T(8,128)(2,1)} %bitcast.4.maps), custom_call_target="tpu_custom_call" | custom-call | flops 268435456 | bytes 8388608 | tf_op jit(solution)/shard_map/expand/pallas_call | solution.py:80
Async XLA Ops:
  128.8 135.4 %all-to-all-start = ((bf16[64,64,512]{2,1,0:T(8,128)(2,1)}), bf16[64,64,512]{2,1,0:T(8,128)(2,1)}, u32[]{:S(2)}, u32[]{:S(2)}) async-start(bf16[64,64,512]{2,1,0:T(8,128)(2,1)} %pack.2), calls=%async_computation | async-start | bytes 8388608 | tf_op jit(solution)/shard_map/all_to_all | solution.py:110
  264.2 6.1 %copy-start.3 = (s32[16]{0:T(128)S(1)}, s32[16]{0:T(128)}, u32[]{:S(2)}) copy-start(s32[16]{0:T(128)} %param.11) | copy-start | bytes 196
  264.3 6.7 %copy-start.2 = (s32[64,1]{0,1:T(1,128)S(1)}, s32[64,1]{0,1:T(1,128)}, u32[]{:S(2)}) copy-start(s32[64,1]{0,1:T(1,128)} %param.10) | copy-start | bytes 772
  264.3 98.5 %all-to-all-start.1 = ((bf16[64,64,512]{2,1,0:T(8,128)(2,1)}), bf16[64,64,512]{2,1,0:T(8,128)(2,1)}, u32[]{:S(2)}, u32[]{:S(2)}) async-start(bf16[64,64,512]{2,1,0:T(8,128)(2,1)} %pack.3), calls=%async_computation.1 | async-start | bytes 8388608 | tf_op jit(solution)/shard_map/all_to_all | solution.py:110
  271.0 2.2 copy-start
  273.2 89.6 %copy-start.1 = (f32[32]{0:T(128)S(1)}, f32[32]{0:T(128)}, u32[]{:S(2)}) copy-start(f32[32]{0:T(128)} %scales.1) | copy-start | bytes 388

commit v2 on v0

v2 whole, which is shorter than its diff:
```python
import functools

import jax
import jax.numpy as jnp
from jax import lax
from jax.experimental import pallas as pl
from jax.experimental.pallas import tpu as pltpu
from jax.sharding import PartitionSpec as P

BLOCK = 64
ROWS = 16
PLANE = 4
VMEM_BYTES = 60 * 2**20

SMEM = pl.BlockSpec(memory_space=pltpu.SMEM)
VMEM = pl.BlockSpec(memory_space=pltpu.VMEM)
HBM = pl.BlockSpec(memory_space=pl.ANY)


SMALL = pl.CostEstimate(flops=0, bytes_accessed=1024, transcendentals=0)


def lists_kernel(dims, caps, where, known, lists, places, pick, slot):
    groups, planes, adapters, stride, own = dims
    plane_blocks = PLANE * own
    blocks = planes * plane_blocks
    row = blocks + planes * PLANE
    my_plane, my_group = where[0], where[1]

    def clear_slot(i, carry):
        slot[i] = -1
        return carry

    def clear_list(i, carry):
        lists[i] = 0
        return carry

    lax.fori_loop(0, planes * adapters, clear_slot, 0)
    lax.fori_loop(0, planes * stride, clear_list, 0)

    def one_plane(plane, largest):
        def one_group(group, found):
            base = lax.rem(my_group - group + groups, groups) * row

            def one_shard(shard, found):
                count = known[base + blocks + plane * PLANE + shard]
                for k in range(own):
                    adapter = known[base + plane * plane_blocks + shard * own + k]
                    at = plane * adapters + adapter
                    held = slot[at]
                    new = jnp.logical_and(count > k * BLOCK, held < 0)
                    slot[at] = jnp.where(new, found, held)
                    lists[plane * stride + found] = jnp.where(new, adapter, 0)
                    found = found + new.astype(jnp.int32)
                return found

            return lax.fori_loop(0, PLANE, one_shard, found)

        return jnp.maximum(largest, lax.fori_loop(0, groups, one_group, 0))

    largest = lax.fori_loop(0, planes, one_plane, 0)
    branch = jnp.int32(0)
    for cap in caps[:-1]:
        branch = branch + (largest > cap).astype(jnp.int32)
    pick[0] = branch

    def one_place(i, carry):
        group, block = i // plane_blocks, lax.rem(i, plane_blocks)
        base = lax.rem(my_group - group + groups, groups) * row
        adapter = known[base + my_plane * plane_blocks + block]
        places[i] = jnp.maximum(slot[my_plane * adapters + adapter], 0)
        return carry

    lax.fori_loop(0, groups * plane_blocks, one_place, 0)


def make_lists(dims, caps, where, known):
    groups, planes, adapters, stride, own = dims
    ints = lambda n: jax.ShapeDtypeStruct((n,), jnp.int32)
    return pl.pallas_call(
        functools.partial(lists_kernel, dims, caps),
        out_shape=(ints(planes * stride), ints(groups * PLANE * own), ints(1)),
        in_specs=[SMEM, SMEM],
        out_specs=(SMEM, SMEM, SMEM),
        scratch_shapes=[pltpu.SMEM((planes * adapters,), jnp.int32)],
        name="lists",
    )(where, known)


def spread_kernel(planes, where, ids, panels, *rest):
    outs, sems = rest[:-1], rest[-1]
    own = outs[0].shape[1]
    for t, out in enumerate(outs):
        shard = lax.rem(where[2] + t, PLANE)

        def send(s, carry, out=out, shard=shard, t=t):
            base = (lax.rem(where[0] + s, planes) * PLANE + shard) * own
            for b in range(own):
                pltpu.make_async_copy(panels.at[ids[base + b]], out.at[s, b], sems.at[t]).start()
            return carry

        lax.fori_loop(0, planes, send, 0)
    for t, out in enumerate(outs):
        pltpu.make_async_copy(out, out, sems.at[t]).wait()


def spread(dims, where, ids, panels):
    groups, planes, adapters, stride, own = dims
    out = jax.ShapeDtypeStruct((planes, own, *panels.shape[1:]), panels.dtype)
    return pl.pallas_call(
        functools.partial(spread_kernel, planes),
        out_shape=(out,) * PLANE,
        in_specs=[SMEM, SMEM, VMEM],
        out_specs=(HBM,) * PLANE,
        scratch_shapes=[pltpu.SemaphoreType.DMA((PLANE,))],
        compiler_params=pltpu.CompilerParams(vmem_limit_bytes=VMEM_BYTES),
        cost_estimate=SMALL,
        name="spread",
    )(where, ids, panels)


def regroup_kernel(planes, where, *refs):
    held, out, sem = refs[:PLANE], refs[PLANE], refs[-1]
    for s in range(planes):
        plane = lax.rem(where[0] + s, planes)
        for t in range(PLANE):
            pltpu.make_async_copy(held[t].at[s], out.at[plane, t], sem).start()
    pltpu.make_async_copy(out, out, sem).wait()


def regroup(where, held):
    planes = held[0].shape[0]
    return pl.pallas_call(
        functools.partial(regroup_kernel, planes),
        out_shape=jax.ShapeDtypeStruct((planes, PLANE, *held[0].shape[1:]), held[0].dtype),
        in_specs=[SMEM, *[VMEM] * PLANE],
        out_specs=HBM,
        scratch_shapes=[pltpu.SemaphoreType.DMA],
        compiler_params=pltpu.CompilerParams(vmem_limit_bytes=VMEM_BYTES),
        cost_estimate=SMALL,
        name="regroup",
    )(where, *held)


def plane_pack_kernel(planes, stride, first, where, lists, panels, *rest):
    outs, sems = rest[:-1], rest[-1]
    ranks = outs[0].shape[1]
    mine = pl.ds(pl.multiple_of(first + where[1] * ranks, ranks), ranks)
    for i, out in enumerate(outs):
        base = lax.rem(where[0] + i + 1, planes) * stride

        def send(k, carry, out=out, base=base, i=i):
            pltpu.make_async_copy(panels.at[lists[base + k], mine], out.at[k], sems.at[i]).start()
            return carry

        lax.fori_loop(0, out.shape[0], send, 0)
    for i, out in enumerate(outs):
        pltpu.make_async_copy(out, out, sems.at[i]).wait()


def plane_pack(dims, cap, first, ranks, where, lists, panels):
    groups, planes, adapters, stride, own = dims
    out = jax.ShapeDtypeStruct((cap, ranks // groups, panels.shape[2]), panels.dtype)
    return pl.pallas_call(
        functools.partial(plane_pack_kernel, planes, stride, first),
        out_shape=(out,) * (planes - 1),
        in_specs=[SMEM, SMEM, VMEM],
        out_specs=(HBM,) * (planes - 1),
        scratch_shapes=[pltpu.SemaphoreType.DMA((planes - 1,))],
        compiler_params=pltpu.CompilerParams(vmem_limit_bytes=VMEM_BYTES),
        cost_estimate=SMALL,
        name="plane_pack",
    )(where, lists, panels)


def group_pack_kernel(groups, planes, where, places, *rest):
    got, outs, sems = rest[: planes - 1], rest[planes - 1 : -1], rest[-1]
    blocks = outs[0].shape[0]
    for i, out in enumerate(outs):
        base = lax.rem(where[1] + i + 1, groups) * blocks

        def send(j, carry, out=out, base=base, i=i):
            place = places[base + j]
            for s in range(planes - 1):
                pltpu.make_async_copy(got[s].at[place], out.at[j, s], sems.at[i]).start()
            return carry

        lax.fori_loop(0, blocks, send, 0)
    for i, out in enumerate(outs):
        pltpu.make_async_copy(out, out, sems.at[i]).wait()


def group_pack(dims, where, places, got):
    groups, planes, adapters, stride, own = dims
    out = jax.ShapeDtypeStruct((PLANE * own, planes - 1, *got[0].shape[1:]), got[0].dtype)
    return pl.pallas_call(
        functools.partial(group_pack_kernel, groups, planes),
        out_shape=(out,) * (groups - 1),
        in_specs=[SMEM, SMEM, *[VMEM] * (planes - 1)],
        out_specs=(HBM,) * (groups - 1),
        scratch_shapes=[pltpu.SemaphoreType.DMA((groups - 1,))],
        compiler_params=pltpu.CompilerParams(vmem_limit_bytes=VMEM_BYTES),
        cost_estimate=SMALL,
        name="group_pack",
    )(where, places, *got)


def shard_pack_kernel(groups, planes, first, where, places, ids, panels, *rest):
    got = rest[: planes - 1]
    swapped = rest[planes - 1 : planes + groups - 2]
    outs, sems = rest[planes + groups - 2 : -1], rest[-1]
    own = outs[0].shape[0]
    ranks = got[0].shape[1]
    my_group, my_shard = where[1], where[2]

    def part(group):
        return pl.ds(pl.multiple_of(group * ranks, ranks), ranks)

    for t, out in enumerate(outs):
        shard = lax.rem(my_shard + t, PLANE)

        def send(b, carry, out=out, shard=shard, t=t):
            j = shard * own + b
            place = places[my_group * PLANE * own + j]
            copy = lambda src, dst: pltpu.make_async_copy(src, dst, sems.at[t]).start()
            copy(panels.at[ids[j], pl.ds(first, out.shape[2])], out.at[b, 0])
            for s in range(planes - 1):
                copy(got[s].at[place], out.at[b, s + 1, part(my_group)])
            for d in range(groups - 1):
                other = lax.rem(my_group + groups - d - 1, groups)
                copy(swapped[d].at[j], out.at[b, pl.ds(1, planes - 1), part(other)])
            return carry

        lax.fori_loop(0, own, send, 0)
    for t, out in enumerate(outs):
        pltpu.make_async_copy(out, out, sems.at[t]).wait()


def shard_pack(dims, first, ranks, where, places, ids, panels, got, swapped):
    groups, planes, adapters, stride, own = dims
    out = jax.ShapeDtypeStruct((own, planes, ranks, panels.shape[2]), panels.dtype)
    return pl.pallas_call(
        functools.partial(shard_pack_kernel, groups, planes, first),
        out_shape=(out,) * PLANE,
        in_specs=[SMEM, SMEM, SMEM, VMEM, *[VMEM] * (planes + groups - 2)],
        out_specs=(HBM,) * PLANE,
        scratch_shapes=[pltpu.SemaphoreType.DMA((PLANE,))],
        compiler_params=pltpu.CompilerParams(vmem_limit_bytes=VMEM_BYTES),
        cost_estimate=SMALL,
        name="shard_pack",
    )(where, places, ids, panels, *got, *swapped)


def shrink_kernel(planes, where, tokens, *rest):
    maps, out = rest[:-1], rest[-1]
    width = maps[0].shape[-1]
    total = jnp.zeros(out.shape, jnp.float32)
    for t in range(PLANE):
        shard = lax.rem(where[2] + PLANE - t, PLANE)
        for s in range(planes):
            source = lax.rem(where[0] + planes - s, planes) * PLANE + shard
            total += lax.dot_general(
                tokens[:, pl.ds(pl.multiple_of(source * width, width), width)],
                jnp.concatenate([m[0, s] for m in maps[t::PLANE]], axis=0),
                (((1,), (1,)), ((), ())),
                preferred_element_type=jnp.float32,
            )
    out[...] = total.astype(out.dtype)


def shrink(where, tokens, maps):
    own, planes, ranks, width = maps[0].shape
    rank = len(maps) // PLANE * ranks
    return pl.pallas_call(
        functools.partial(shrink_kernel, planes),
        grid=(own,),
        out_shape=jax.ShapeDtypeStruct((own * BLOCK, rank), tokens.dtype),
        in_specs=[
            SMEM,
            pl.BlockSpec((BLOCK, tokens.shape[1]), lambda b: (b, 0)),
            *[pl.BlockSpec((1, planes, ranks, width), lambda b: (b, 0, 0, 0))] * len(maps),
        ],
        out_specs=pl.BlockSpec((BLOCK, rank), lambda b: (b, 0)),
        compiler_params=pltpu.CompilerParams(vmem_limit_bytes=VMEM_BYTES),
        cost_estimate=SMALL,
        name="shrink",
    )(where, tokens, *maps)


def expand_kernel(planes, where, ids, count, scales, shrunk, maps, out):
    b = pl.program_id(0)
    scale = scales[ids[b]]
    width = maps.shape[-1]
    rows = b * BLOCK + lax.broadcasted_iota(jnp.int32, (BLOCK, width), 0)
    live = rows < count[0]
    for plane in range(planes):
        for t in range(PLANE):
            source = plane * PLANE + lax.rem(where[2] + PLANE - t, PLANE)
            part = jnp.dot(shrunk[...], maps[plane, t, 0], preferred_element_type=jnp.float32)
            columns = pl.ds(pl.multiple_of(source * width, width), width)
            out[:, columns] = jnp.where(live, part * scale, 0.0).astype(out.dtype)


def expand(where, ids, count, scales, shrunk, maps):
    planes, _, own, rank, width = maps.shape
    columns = planes * PLANE * width
    return pl.pallas_call(
        functools.partial(expand_kernel, planes),
        grid=(own,),
        out_shape=jax.ShapeDtypeStruct((own * BLOCK, columns), shrunk.dtype),
        in_specs=[
            *[SMEM] * 4,
            pl.BlockSpec((BLOCK, rank), lambda b: (b, 0)),
            pl.BlockSpec((planes, PLANE, 1, rank, width), lambda b: (0, 0, b, 0, 0)),
        ],
        out_specs=pl.BlockSpec((BLOCK, columns), lambda b: (b, 0)),
        compiler_params=pltpu.CompilerParams(vmem_limit_bytes=VMEM_BYTES),
        cost_estimate=SMALL,
        name="expand",
    )(where, ids, count, scales, shrunk, maps)


def body(groups, tokens, shrink_panels, expand_panels, adapter_scale, block_adapter, shard_counts):
    devices = shard_counts.shape[0]
    own = tokens.shape[0] // BLOCK
    planes = devices // PLANE
    adapters = shrink_panels.shape[0]
    most = min(adapters, groups * PLANE * own)
    dims = (groups, planes, adapters, most + 1, own)
    caps = tuple(most * part // 16 for part in (8, 9, 10, 11, 13, 16))

    ids = block_adapter.reshape(-1)
    me, group = lax.axis_index("blk"), lax.axis_index("groups")
    where = jnp.stack([me // PLANE, group, lax.rem(me, PLANE)]).astype(jnp.int32)
    facts = jnp.concatenate([ids, shard_counts])
    known = [facts]
    for d in range(1, groups):
        known.append(lax.ppermute(facts, "groups", [(i, (i + d) % groups) for i in range(groups)]))
    lists, places, pick = make_lists(dims, caps, where, jnp.concatenate(known))
    plane_ids = lax.dynamic_slice_in_dim(ids, me // PLANE * PLANE * own, PLANE * own, 0)
    mine = lax.dynamic_slice_in_dim(ids, me * own, own, 0)
    count = lax.dynamic_slice_in_dim(shard_counts, me, 1, 0)
    down_panels = jnp.swapaxes(shrink_panels, 1, 2)

    def plane_shift(x, s):
        return lax.ppermute(x, "blk", [(i, (i + s * PLANE) % devices) for i in range(devices)])

    def group_shift(x, d):
        return lax.ppermute(x, "groups", [(i, (i + d) % groups) for i in range(groups)])

    def shard_shift(x, t):
        pairs = [(i, i // PLANE * PLANE + (i + t) % PLANE) for i in range(devices)]
        return lax.ppermute(x, "blk", pairs)

    rank = expand_panels.shape[1]
    parts = 2 if rank % (2 * groups * ROWS) == 0 else 1
    ranks = rank // parts

    up_sent = spread(dims, where, ids, expand_panels)

    def run(cap):
        def branch(up_sent):
            sent = [plane_pack(dims, cap, h * ranks, ranks, where, lists, down_panels) for h in range(parts)]
            near = [up_sent[0], *[shard_shift(up_sent[t], t) for t in range(1, PLANE)]]
            up_packed = regroup(where, near)
            got, maps = [], []
            for h in range(parts):
                got.append([plane_shift(x, s + 1) for s, x in enumerate(sent[h])])
                if h + 1 < parts:
                    got[h], sent[h + 1] = lax.optimization_barrier((got[h], sent[h + 1]))
                else:
                    got[h], up_packed = lax.optimization_barrier((got[h], up_packed))
                swaps = group_pack(dims, where, places, got[h])
                swapped = [group_shift(x, d + 1) for d, x in enumerate(swaps)]
                maps.append(
                    shard_pack(dims, h * ranks, ranks, where, places, plane_ids, down_panels, got[h], swapped)
                )
            mirrors = [list(range(i, devices, PLANE)) for i in range(PLANE)]
            up = lax.all_to_all(up_packed, "blk", split_axis=0, concat_axis=0, tiled=True, axis_index_groups=mirrors)
            down = []
            for kept, *moved in maps:
                down += [kept, *[shard_shift(x, t + 1) for t, x in enumerate(moved)]]
            shrunk = shrink(where, tokens, down)
            return expand(where, mine, count, adapter_scale, shrunk, up)

        return branch

    return lax.switch(pick[0], [run(cap) for cap in caps], up_sent)


def solution(mesh):
    return jax.shard_map(
        functools.partial(body, mesh.shape["groups"]),
        mesh=mesh,
        in_specs=(
            P(("groups", "blk"), None),
            P(None, "blk", None),
            P(None, None, "blk"),
            P(),
            P("groups", None),
            P("groups"),
        ),
        out_specs=P(("groups", "blk"), None),
        check_vma=False,
    )
```

time: 229 us -> 181 us (0.79)
  the two profiles are of different devices: /device:TPU:13 before, /device:TPU:0 now
where the time goes in v2:
time: 181 us; the launch traced here: 183 us
  waiting for transfers between devices  99.5 us (55%)
  Pallas kernels  40.2 us (22%)
  starting transfers between devices  36.5 us (20%)
  local copies, waits for them, and re-layouts  3.64 us (2%)
  other arithmetic  2.13 us (1%)
    ppermute x6, waiting for transfers between devices, plane_shift(): lax.ppermute(x, 'blk', [(i, (i + s * PLANE) % devices) for i in range(dev...  33.7 us
    ppermute x9, waiting for transfers between devices, shard_shift(): return lax.ppermute(x, 'blk', pairs)  29.1 us
    ppermute x2, waiting for transfers between devices, group_shift(): lax.ppermute(x, 'groups', [(i, (i + d) % groups) for i in range(groups)])  23.9 us
    ppermute x6, starting transfers between devices, plane_shift(): lax.ppermute(x, 'blk', [(i, (i + s * PLANE) % devices) for i in range(dev...  12.7 us
    all_to_all x1, waiting for transfers between devices, branch(): lax.all_to_all(up_packed, 'blk', split_axis=0, concat_axis=0, tiled=True,...  12.7 us
    ppermute x9, starting transfers between devices, shard_shift(): return lax.ppermute(x, 'blk', pairs)  11.2 us
    all_to_all x1, starting transfers between devices, branch(): lax.all_to_all(up_packed, 'blk', split_axis=0, concat_axis=0, tiled=True,...  7.48 us
    pallas_call x1, Pallas kernels, expand(): pl.pallas_call(functools.partial(expand_kernel, planes), grid=(own,), out...  6.13 us
  transfers between devices with their start and end apart: 19, of which 12 were waited for; matrix products, arithmetic and copies ran while one was open for 1% of the time, Pallas kernels for 16%

profile of v2, /device:TPU:0, one launch (start us, length us, event | category | flops | bytes accessed | tf_op | source)
XLA Modules:
  0.0 182.7 jit_solution(11901165081458621279)
XLA Ops:
  0.7 2.9 %collective-permute-start.102 = (s32[80]{0:T(128)S(1)}, s32[80]{0:T(128)S(1)}, u32[]{:S(2)}, u32[]{:S(2)}) collective-permute-start(s32[80]{0:T(128)S(1)} %pad_add_fusion.2), channel_id=1, source_target_pairs={{0,16},{16,0},{1,17},{17,1},{2,18},{18,2},{3,19},{19,3},{4,20},{20... | collective-permute-start | bytes 968 | tf_op jit(solution)/shard_map/ppermute | solution.py:338
  3.8 4.8 %spread.1 = (bf16[4,4,64,512]{3,2,1,0:T(8,128)(2,1)S(1)}, bf16[4,4,64,512]{3,2,1,0:T(8,128)(2,1)}, bf16[4,4,64,512]{3,2,1,0:T(8,128)(2,1)}, bf16[4,4,64,512]{3,2,1,0:T(8,128)(2,1)}) custom-call(s32[3]{0:T(128)S(1)} %pad_add_fusion.1.where, s32[64]{0:T(128)} %bitcast.37, bf16[32,64,512]{2,1,0:T(8,128)(2,1)} %panels.1), custom_call_target="tpu_custom_call" | custom-call | bytes 1024 | tf_op jit(solution)/shard_map/spread/pallas_call | solution.py:110
  9.9 4.8 %lists.1 = (s32[132]{0:T(256)S(1)}, s32[32]{0:T(128)S(1)}, s32[1]{0:T(128)}) custom-call(s32[3]{0:T(128)S(1)} %pad_add_fusion.1.where, s32[160]{0:T(256)} %pad_add_fusion.known), custom_call_target="tpu_custom_call" | custom-call | tf_op jit(solution)/shard_map/lists/pallas_call | solution.py:80
  15.4 167.4 %conditional.1 = (bf16[256,8192]{1,0:T(8,128)(2,1)}) conditional(s32[]{:T(128)} %bitcast.16, (s32[3]{0:T(128)S(1)}, s32[132]{0:T(256)S(1)}, bf16[32,64,512]{2,1,0:T(8,128)(2,1)}, s32[32]{0:T(128)S(1)}, s32[64,1]{0,1:T(1,128)}, /*index=5*/bf16[4,4,64,512]{3,2,1,0:T(8,128)(2,1)}, bf16[4,4,64,512]{3,2,1,0:T(8,128)(2,1)}, ...), branch_computations={%region_0.1_spmd, %region_1.2_spmd, %region_2.3_spmd, %region_3.4_... | conditional | flops 8 | bytes 84947024 | solution.py:388
  25.3 8.6 %collective-permute-done.34.rest_0_ = bf16[20,16,512]{2,1,0:T(8,128)(2,1)S(1)} collective-permute-done((bf16[20,16,512]{2,1,0:T(8,128)(2,1)}, bf16[20,16,512]{2,1,0:T(8,128)(2,1)S(1)}, u32[]{:S(2)}, u32[]{:S(2)}) %collective-permute-start.34) | collective-permute-done | bytes 327712 | tf_op jit(solution)/shard_map/cond/branch_2_fun/ppermute | solution.py:346
  34.4 2.7 %plane_pack.17 = (bf16[20,16,512]{2,1,0:T(8,128)(2,1)}, bf16[20,16,512]{2,1,0:T(8,128)(2,1)}, bf16[20,16,512]{2,1,0:T(8,128)(2,1)}) custom-call(s32[3]{0:T(128)S(1)} %get-tuple-element.242.where, s32[132]{0:T(256)S(1)} %get-tuple-element.250.lists, bf16[32,64,512]{2,1,0:T(8,128)(2,1)} %get-tuple-element.249.panels), custom_call_target="tpu_custom_call" | custom-call | bytes 1024 | tf_op jit(solution)/shard_map/cond/branch_2_fun/plane_pack/pallas_call | solution.py:164
  37.1 9.1 %collective-permute-done.35.rest_1_ = bf16[20,16,512]{2,1,0:T(8,128)(2,1)S(1)} collective-permute-done((bf16[20,16,512]{2,1,0:T(8,128)(2,1)}, bf16[20,16,512]{2,1,0:T(8,128)(2,1)S(1)}, u32[]{:S(2)}, u32[]{:S(2)}) %collective-permute-start.35) | collective-permute-done | bytes 327712 | tf_op jit(solution)/shard_map/cond/branch_2_fun/ppermute | solution.py:346
  46.1 6.0 %collective-permute-done.36.rest_2_ = bf16[20,16,512]{2,1,0:T(8,128)(2,1)S(1)} collective-permute-done((bf16[20,16,512]{2,1,0:T(8,128)(2,1)}, bf16[20,16,512]{2,1,0:T(8,128)(2,1)S(1)}, u32[]{:S(2)}, u32[]{:S(2)}) %collective-permute-start.36) | collective-permute-done | bytes 327712 | tf_op jit(solution)/shard_map/cond/branch_2_fun/ppermute | solution.py:346
  54.5 2.8 %collective-permute-start.42 = (bf16[20,16,512]{2,1,0:T(8,128)(2,1)}, bf16[20,16,512]{2,1,0:T(8,128)(2,1)}, u32[]{:S(2)}, u32[]{:S(2)}) collective-permute-start(bf16[20,16,512]{2,1,0:T(8,128)(2,1)} %get-tuple-element.265), channel_id=1, source_target_pairs={{0,8},{1,9},{2,10},{3,11},{4,12},{5,13},{6,14},{7,15},{8,0},{9,1},... | collective-permute-start | bytes 983048 | tf_op jit(solution)/shard_map/cond/branch_2_fun/ppermute | solution.py:346
  57.3 2.9 %collective-permute-start.43 = (bf16[20,16,512]{2,1,0:T(8,128)(2,1)}, bf16[20,16,512]{2,1,0:T(8,128)(2,1)}, u32[]{:S(2)}, u32[]{:S(2)}) collective-permute-start(bf16[20,16,512]{2,1,0:T(8,128)(2,1)} %get-tuple-element.266), channel_id=1, source_target_pairs={{0,12},{1,13},{2,14},{3,15},{4,0},{5,1},{6,2},{7,3},{8,4},{9,5},{1... | collective-permute-start | bytes 983048 | tf_op jit(solution)/shard_map/cond/branch_2_fun/ppermute | solution.py:346
  62.7 3.9 %regroup.8 = bf16[4,4,4,64,512]{4,3,2,1,0:T(8,128)(2,1)} custom-call(s32[3]{0:T(128)S(1)} %get-tuple-element.242.where, bf16[4,4,64,512]{3,2,1,0:T(8,128)(2,1)S(1)} %get-tuple-element.267.refs_0_, bf16[4,4,64,512]{3,2,1,0:T(8,128)(2,1)} %copy-done.24, bf16[4,4,64,512]{3,2,1,0:T(8,128)(2,1)} %collective-permute-done.45.refs_2_, ...), custom_call_target="tpu_custom_call" | custom-call | bytes 1024 | tf_op jit(solution)/shard_map/cond/branch_2_fun/regroup/pallas_call | solution.py:133
  66.7 10.1 %collective-permute-done.42.rest_1_ = bf16[20,16,512]{2,1,0:T(8,128)(2,1)} collective-permute-done((bf16[20,16,512]{2,1,0:T(8,128)(2,1)}, bf16[20,16,512]{2,1,0:T(8,128)(2,1)}, u32[]{:S(2)}, u32[]{:S(2)}) %collective-permute-start.42) | collective-permute-done | bytes 327712 | tf_op jit(solution)/shard_map/cond/branch_2_fun/ppermute | solution.py:346
  76.8 7.5 %all-to-all-start.2 = ((bf16[4,4,4,64,512]{4,3,2,1,0:T(8,128)(2,1)}), bf16[4,4,4,64,512]{4,3,2,1,0:T(8,128)(2,1)}, u32[]{:S(2)}, u32[]{:S(2)}) async-start(bf16[4,4,4,64,512]{4,3,2,1,0:T(8,128)(2,1)} %regroup.8), calls=%async_computation.2 | async-start | bytes 8388608 | tf_op jit(solution)/shard_map/cond/branch_2_fun/all_to_all | solution.py:379
  91.2 16.0 %collective-permute-done.37.rest_3_ = bf16[16,3,16,512]{3,2,1,0:T(8,128)(2,1)} collective-permute-done((bf16[16,3,16,512]{3,2,1,0:T(8,128)(2,1)}, bf16[16,3,16,512]{3,2,1,0:T(8,128)(2,1)}, u32[]{:S(2)}, u32[]{:S(2)}) %collective-permute-start.37) | collective-permute-done | bytes 786464 | tf_op jit(solution)/shard_map/cond/branch_2_fun/ppermute | solution.py:349
  107.2 2.8 %shard_pack.16 = (bf16[4,4,32,512]{3,2,1,0:T(8,128)(2,1)}, bf16[4,4,32,512]{3,2,1,0:T(8,128)(2,1)}, bf16[4,4,32,512]{3,2,1,0:T(8,128)(2,1)}, bf16[4,4,32,512]{3,2,1,0:T(8,128)(2,1)}) custom-call(s32[3]{0:T(128)S(1)} %get-tuple-element.242.where, s32[32]{0:T(128)S(1)} %get-tuple-element.247.places, s32[16]{0:T(128)} %fusion.5.ids, ...), custom_call_target="tpu_custom_call" | custom-call | bytes 1024 | tf_op jit(solution)/shard_map/cond/branch_2_fun/shard_pack/pallas_call | solution.py:242
  113.4 7.9 %collective-permute-done.47.rest_3_ = bf16[16,3,16,512]{3,2,1,0:T(8,128)(2,1)S(1)} collective-permute-done((bf16[16,3,16,512]{3,2,1,0:T(8,128)(2,1)}, bf16[16,3,16,512]{3,2,1,0:T(8,128)(2,1)S(1)}, u32[]{:S(2)}, u32[]{:S(2)}) %collective-permute-start.47) | collective-permute-done | bytes 786464 | tf_op jit(solution)/shard_map/cond/branch_2_fun/ppermute | solution.py:349
  122.3 2.8 %shard_pack.17 = (bf16[4,4,32,512]{3,2,1,0:T(8,128)(2,1)}, bf16[4,4,32,512]{3,2,1,0:T(8,128)(2,1)}, bf16[4,4,32,512]{3,2,1,0:T(8,128)(2,1)}, bf16[4,4,32,512]{3,2,1,0:T(8,128)(2,1)}) custom-call(s32[3]{0:T(128)S(1)} %get-tuple-element.242.where, s32[32]{0:T(128)S(1)} %get-tuple-element.247.places, s32[16]{0:T(128)} %fusion.5.ids, ...), custom_call_target="tpu_custom_call" | custom-call | bytes 1024 | tf_op jit(solution)/shard_map/cond/branch_2_fun/shard_pack/pallas_call | solution.py:242
  125.2 3.3 %collective-permute-start.49 = (bf16[4,4,32,512]{3,2,1,0:T(8,128)(2,1)}, bf16[4,4,32,512]{3,2,1,0:T(8,128)(2,1)S(1)}, u32[]{:S(2)}, u32[]{:S(2)}) collective-permute-start(bf16[4,4,32,512]{3,2,1,0:T(8,128)(2,1)} %get-tuple-element.276), channel_id=1, source_target_pairs={{0,2},{1,3},{2,0},{3,1},{4,6},{5,7},{6,4},{7,5},{8,10},{9,11},{10,... | collective-permute-start | bytes 1572872 | tf_op jit(solution)/shard_map/cond/branch_2_fun/ppermute | solution.py:353
  131.2 4.7 %collective-permute-done.40.rest_3_ = bf16[4,4,32,512]{3,2,1,0:T(8,128)(2,1)} collective-permute-done((bf16[4,4,32,512]{3,2,1,0:T(8,128)(2,1)}, bf16[4,4,32,512]{3,2,1,0:T(8,128)(2,1)}, u32[]{:S(2)}, u32[]{:S(2)}) %collective-permute-start.40) | collective-permute-done | bytes 524320 | tf_op jit(solution)/shard_map/cond/branch_2_fun/ppermute | solution.py:353
  135.9 10.5 %collective-permute-done.48.rest_5_ = bf16[4,4,32,512]{3,2,1,0:T(8,128)(2,1)S(1)} collective-permute-done((bf16[4,4,32,512]{3,2,1,0:T(8,128)(2,1)}, bf16[4,4,32,512]{3,2,1,0:T(8,128)(2,1)S(1)}, u32[]{:S(2)}, u32[]{:S(2)}) %collective-permute-start.48) | collective-permute-done | bytes 524320 | tf_op jit(solution)/shard_map/cond/branch_2_fun/ppermute | solution.py:353
  147.6 10.1 %collective-permute-done.50.rest_7_ = bf16[4,4,32,512]{3,2,1,0:T(8,128)(2,1)S(1)} collective-permute-done((bf16[4,4,32,512]{3,2,1,0:T(8,128)(2,1)}, bf16[4,4,32,512]{3,2,1,0:T(8,128)(2,1)S(1)}, u32[]{:S(2)}, u32[]{:S(2)}) %collective-permute-start.50) | collective-permute-done | bytes 524320 | tf_op jit(solution)/shard_map/cond/branch_2_fun/ppermute | solution.py:353
  158.5 5.4 %shrink.8.shrunk = bf16[256,64]{1,0:T(8,128)(2,1)} custom-call(s32[3]{0:T(128)S(1)} %get-tuple-element.242.where, bf16[256,8192]{1,0:T(8,128)(2,1)} %get-tuple-element.461.tokens, bf16[4,4,32,512]{3,2,1,0:T(8,128)(2,1)} %get-tuple-element.260.rest_0_, bf16[4,4,32,512]{3,2,1,0:T(8,128)(2,1)} %collective-permute-done.38.rest_1_, ...), custom_call_target="tpu_custom_call" | custom-call | bytes 1024 | tf_op jit(solution)/shard_map/cond/branch_2_fun/shrink/pallas_call | solution.py:274
  163.9 12.7 %all-to-all-done.2.maps = bf16[4,4,4,64,512]{4,3,2,1,0:T(8,128)(2,1)} async-done(((bf16[4,4,4,64,512]{4,3,2,1,0:T(8,128)(2,1)}), bf16[4,4,4,64,512]{4,3,2,1,0:T(8,128)(2,1)}, u32[]{:S(2)}, u32[]{:S(2)}) %all-to-all-start.2) | async-done | bytes 4194336 | tf_op jit(solution)/shard_map/cond/branch_2_fun/all_to_all | solution.py:379
  176.6 6.1 %expand.8 = bf16[256,8192]{1,0:T(8,128)(2,1)} custom-call(s32[3]{0:T(128)S(1)} %get-tuple-element.242.where, s32[4]{0:T(128)} %fusion.4.ids, s32[1]{0:T(128)} %dynamic_slice.32.count, f32[32]{0:T(128)S(1)} %copy-done.57, bf16[256,64]{1,0:T(8,128)(2,1)} %shrink.8.shrunk, bf16[4,4,4,64,512]{4,3,2,1,0:T(8,128)(2,1)} %all-to-all-done.2.maps), custom_call_target="tpu_custom_call" | custom-call | bytes 1024 | tf_op jit(solution)/shard_map/cond/branch_2_fun/expand/pallas_call | solution.py:307
  (56 shorter events, 33.4 us)
Async XLA Ops:
  0.7 7.8 %collective-permute-start.102 = (s32[80]{0:T(128)S(1)}, s32[80]{0:T(128)S(1)}, u32[]{:S(2)}, u32[]{:S(2)}) collective-permute-start(s32[80]{0:T(128)S(1)} %pad_add_fusion.2), channel_id=1, source_target_pairs={{0,16},{16,0},{1,17},{17,1},{2,18},{18,2},{3,19},{19,3},{4,20},{20... | collective-permute-start | bytes 968 | tf_op jit(solution)/shard_map/ppermute | solution.py:338
  15.4 41.9 %collective-permute-start.44 = (bf16[4,4,64,512]{3,2,1,0:T(8,128)(2,1)}, bf16[4,4,64,512]{3,2,1,0:T(8,128)(2,1)S(1)}, u32[]{:S(2)}, u32[]{:S(2)}) collective-permute-start(bf16[4,4,64,512]{3,2,1,0:T(8,128)(2,1)} %get-tuple-element.268), channel_id=1, source_target_pairs={{0,1},{1,2},{2,3},{3,0},{4,5},{5,6},{6,7},{7,4},{8,9},{9,10},{10,1... | collective-permute-start | bytes 3145736 | tf_op jit(solution)/shard_map/cond/branch_2_fun/ppermute | solution.py:353
  15.5 44.7 %collective-permute-start.45 = (bf16[4,4,64,512]{3,2,1,0:T(8,128)(2,1)}, bf16[4,4,64,512]{3,2,1,0:T(8,128)(2,1)}, u32[]{:S(2)}, u32[]{:S(2)}) collective-permute-start(bf16[4,4,64,512]{3,2,1,0:T(8,128)(2,1)} %get-tuple-element.269), channel_id=1, source_target_pairs={{0,2},{1,3},{2,0},{3,1},{4,6},{5,7},{6,4},{7,5},{8,10},{9,11},{10,... | collective-permute-start | bytes 3145736 | tf_op jit(solution)/shard_map/cond/branch_2_fun/ppermute | solution.py:353
  17.0 45.7 %collective-permute-start.46 = (bf16[4,4,64,512]{3,2,1,0:T(8,128)(2,1)}, bf16[4,4,64,512]{3,2,1,0:T(8,128)(2,1)}, u32[]{:S(2)}, u32[]{:S(2)}) collective-permute-start(bf16[4,4,64,512]{3,2,1,0:T(8,128)(2,1)} %get-tuple-element.270), channel_id=1, source_target_pairs={{0,3},{1,0},{2,1},{3,2},{4,7},{5,4},{6,5},{7,6},{8,11},{9,8},{10,9... | collective-permute-start | bytes 3145736 | tf_op jit(solution)/shard_map/cond/branch_2_fun/ppermute | solution.py:353
  21.1 12.8 %collective-permute-start.34 = (bf16[20,16,512]{2,1,0:T(8,128)(2,1)}, bf16[20,16,512]{2,1,0:T(8,128)(2,1)S(1)}, u32[]{:S(2)}, u32[]{:S(2)}) collective-permute-start(bf16[20,16,512]{2,1,0:T(8,128)(2,1)} %get-tuple-element.251), channel_id=1, source_target_pairs={{0,4},{1,5},{2,6},{3,7},{4,8},{5,9},{6,10},{7,11},{8,12},{9,13},{1... | collective-permute-start | bytes 983048 | tf_op jit(solution)/shard_map/cond/branch_2_fun/ppermute | solution.py:346
  22.7 23.4 %collective-permute-start.35 = (bf16[20,16,512]{2,1,0:T(8,128)(2,1)}, bf16[20,16,512]{2,1,0:T(8,128)(2,1)S(1)}, u32[]{:S(2)}, u32[]{:S(2)}) collective-permute-start(bf16[20,16,512]{2,1,0:T(8,128)(2,1)} %get-tuple-element.252), channel_id=1, source_target_pairs={{0,8},{1,9},{2,10},{3,11},{4,12},{5,13},{6,14},{7,15},{8,0},{9,1},... | collective-permute-start | bytes 983048 | tf_op jit(solution)/shard_map/cond/branch_2_fun/ppermute | solution.py:346
  33.9 32.7 %copy-start.16 = (bf16[20,16,512]{2,1,0:T(8,128)(2,1)}, bf16[20,16,512]{2,1,0:T(8,128)(2,1)S(1)}, u32[]{:S(2)}) copy-start(bf16[20,16,512]{2,1,0:T(8,128)(2,1)S(1)} %collective-permute-done.34.rest_0_) | copy-start | bytes 983044 | tf_op jit(solution)/shard_map/cond
  33.9 18.2 %collective-permute-start.36 = (bf16[20,16,512]{2,1,0:T(8,128)(2,1)}, bf16[20,16,512]{2,1,0:T(8,128)(2,1)S(1)}, u32[]{:S(2)}, u32[]{:S(2)}) collective-permute-start(bf16[20,16,512]{2,1,0:T(8,128)(2,1)} %get-tuple-element.253), channel_id=1, source_target_pairs={{0,12},{1,13},{2,14},{3,15},{4,0},{5,1},{6,2},{7,3},{8,4},{9,5},{1... | collective-permute-start | bytes 983048 | tf_op jit(solution)/shard_map/cond/branch_2_fun/ppermute | solution.py:346
  46.1 20.5 %copy-start.17 = (bf16[20,16,512]{2,1,0:T(8,128)(2,1)}, bf16[20,16,512]{2,1,0:T(8,128)(2,1)S(1)}, u32[]{:S(2)}) copy-start(bf16[20,16,512]{2,1,0:T(8,128)(2,1)S(1)} %collective-permute-done.35.rest_1_) | copy-start | bytes 983044 | tf_op jit(solution)/shard_map/cond
  52.1 14.5 %collective-permute-start.41 = (bf16[20,16,512]{2,1,0:T(8,128)(2,1)}, bf16[20,16,512]{2,1,0:T(8,128)(2,1)}, u32[]{:S(2)}, u32[]{:S(2)}) collective-permute-start(bf16[20,16,512]{2,1,0:T(8,128)(2,1)} %get-tuple-element.264), channel_id=1, source_target_pairs={{0,4},{1,5},{2,6},{3,7},{4,8},{5,9},{6,10},{7,11},{8,12},{9,13},{1... | collective-permute-start | bytes 983048 | tf_op jit(solution)/shard_map/cond/branch_2_fun/ppermute | solution.py:346
  54.5 22.3 %collective-permute-start.42 = (bf16[20,16,512]{2,1,0:T(8,128)(2,1)}, bf16[20,16,512]{2,1,0:T(8,128)(2,1)}, u32[]{:S(2)}, u32[]{:S(2)}) collective-permute-start(bf16[20,16,512]{2,1,0:T(8,128)(2,1)} %get-tuple-element.265), channel_id=1, source_target_pairs={{0,8},{1,9},{2,10},{3,11},{4,12},{5,13},{6,14},{7,15},{8,0},{9,1},... | collective-permute-start | bytes 983048 | tf_op jit(solution)/shard_map/cond/branch_2_fun/ppermute | solution.py:346
  57.3 19.5 %collective-permute-start.43 = (bf16[20,16,512]{2,1,0:T(8,128)(2,1)}, bf16[20,16,512]{2,1,0:T(8,128)(2,1)}, u32[]{:S(2)}, u32[]{:S(2)}) collective-permute-start(bf16[20,16,512]{2,1,0:T(8,128)(2,1)} %get-tuple-element.266), channel_id=1, source_target_pairs={{0,12},{1,13},{2,14},{3,15},{4,0},{5,1},{6,2},{7,3},{8,4},{9,5},{1... | collective-permute-start | bytes 983048 | tf_op jit(solution)/shard_map/cond/branch_2_fun/ppermute | solution.py:346
  66.6 24.0 %copy-start.63 = (s32[64,1]{0,1:T(1,128)S(1)}, s32[64,1]{0,1:T(1,128)}, u32[]{:S(2)}) copy-start(s32[64,1]{0,1:T(1,128)} %get-tuple-element.471) | copy-start | bytes 772 | tf_op jit(solution)/shard_map/cond
  66.6 40.5 %copy-start.2 = (bf16[32,64,512]{2,1,0:T(8,128)(2,1)S(1)}, bf16[32,64,512]{2,1,0:T(8,128)(2,1)}, u32[]{:S(2)}) copy-start(bf16[32,64,512]{2,1,0:T(8,128)(2,1)} %get-tuple-element.249.panels) | copy-start | bytes 6291460 | tf_op jit(solution)/shard_map/cond
  76.8 99.8 %all-to-all-start.2 = ((bf16[4,4,4,64,512]{4,3,2,1,0:T(8,128)(2,1)}), bf16[4,4,4,64,512]{4,3,2,1,0:T(8,128)(2,1)}, u32[]{:S(2)}, u32[]{:S(2)}) async-start(bf16[4,4,4,64,512]{4,3,2,1,0:T(8,128)(2,1)} %regroup.8), calls=%async_computation.2 | async-start | bytes 8388608 | tf_op jit(solution)/shard_map/cond/branch_2_fun/all_to_all | solution.py:379
  86.3 20.9 %collective-permute-start.37 = (bf16[16,3,16,512]{3,2,1,0:T(8,128)(2,1)}, bf16[16,3,16,512]{3,2,1,0:T(8,128)(2,1)}, u32[]{:S(2)}, u32[]{:S(2)}) collective-permute-start(bf16[16,3,16,512]{3,2,1,0:T(8,128)(2,1)} %group_pack.16), channel_id=1, source_target_pairs={{0,16},{16,0},{1,17},{17,1},{2,18},{18,2},{3,19},{19,3},{4,20},{20... | collective-permute-start | bytes 2359304 | tf_op jit(solution)/shard_map/cond/branch_2_fun/ppermute | solution.py:349
  89.0 40.8 %copy-start.69 = (s32[16]{0:T(128)S(1)}, s32[16]{0:T(128)}, u32[]{:S(2)}) copy-start(s32[16]{0:T(128)} %get-tuple-element.427) | copy-start | bytes 196 | tf_op jit(solution)/shard_map/cond
  89.0 32.3 %collective-permute-start.47 = (bf16[16,3,16,512]{3,2,1,0:T(8,128)(2,1)}, bf16[16,3,16,512]{3,2,1,0:T(8,128)(2,1)S(1)}, u32[]{:S(2)}, u32[]{:S(2)}) collective-permute-start(bf16[16,3,16,512]{3,2,1,0:T(8,128)(2,1)} %group_pack.17), channel_id=1, source_target_pairs={{0,16},{16,0},{1,17},{17,1},{2,18},{18,2},{3,19},{19,3},{4,20},{20... | collective-permute-start | bytes 2359304 | tf_op jit(solution)/shard_map/cond/branch_2_fun/ppermute | solution.py:349
  110.0 18.5 %collective-permute-start.38 = (bf16[4,4,32,512]{3,2,1,0:T(8,128)(2,1)}, bf16[4,4,32,512]{3,2,1,0:T(8,128)(2,1)}, u32[]{:S(2)}, u32[]{:S(2)}) collective-permute-start(bf16[4,4,32,512]{3,2,1,0:T(8,128)(2,1)} %get-tuple-element.261), channel_id=1, source_target_pairs={{0,1},{1,2},{2,3},{3,0},{4,5},{5,6},{6,7},{7,4},{8,9},{9,10},{10,1... | collective-permute-start | bytes 1572872 | tf_op jit(solution)/shard_map/cond/branch_2_fun/ppermute | solution.py:353
  110.1 21.1 %collective-permute-start.39 = (bf16[4,4,32,512]{3,2,1,0:T(8,128)(2,1)}, bf16[4,4,32,512]{3,2,1,0:T(8,128)(2,1)}, u32[]{:S(2)}, u32[]{:S(2)}) collective-permute-start(bf16[4,4,32,512]{3,2,1,0:T(8,128)(2,1)} %get-tuple-element.262), channel_id=1, source_target_pairs={{0,2},{1,3},{2,0},{3,1},{4,6},{5,7},{6,4},{7,5},{8,10},{9,11},{10,... | collective-permute-start | bytes 1572872 | tf_op jit(solution)/shard_map/cond/branch_2_fun/ppermute | solution.py:353
  112.0 23.8 %collective-permute-start.40 = (bf16[4,4,32,512]{3,2,1,0:T(8,128)(2,1)}, bf16[4,4,32,512]{3,2,1,0:T(8,128)(2,1)}, u32[]{:S(2)}, u32[]{:S(2)}) collective-permute-start(bf16[4,4,32,512]{3,2,1,0:T(8,128)(2,1)} %get-tuple-element.263), channel_id=1, source_target_pairs={{0,3},{1,0},{2,1},{3,2},{4,7},{5,4},{6,5},{7,6},{8,11},{9,8},{10,9... | collective-permute-start | bytes 1572872 | tf_op jit(solution)/shard_map/cond/branch_2_fun/ppermute | solution.py:353
  125.1 21.2 %collective-permute-start.48 = (bf16[4,4,32,512]{3,2,1,0:T(8,128)(2,1)}, bf16[4,4,32,512]{3,2,1,0:T(8,128)(2,1)S(1)}, u32[]{:S(2)}, u32[]{:S(2)}) collective-permute-start(bf16[4,4,32,512]{3,2,1,0:T(8,128)(2,1)} %get-tuple-element.275), channel_id=1, source_target_pairs={{0,1},{1,2},{2,3},{3,0},{4,5},{5,6},{6,7},{7,4},{8,9},{9,10},{10,1... | collective-permute-start | bytes 1572872 | tf_op jit(solution)/shard_map/cond/branch_2_fun/ppermute | solution.py:353
  125.2 22.4 %collective-permute-start.49 = (bf16[4,4,32,512]{3,2,1,0:T(8,128)(2,1)}, bf16[4,4,32,512]{3,2,1,0:T(8,128)(2,1)S(1)}, u32[]{:S(2)}, u32[]{:S(2)}) collective-permute-start(bf16[4,4,32,512]{3,2,1,0:T(8,128)(2,1)} %get-tuple-element.276), channel_id=1, source_target_pairs={{0,2},{1,3},{2,0},{3,1},{4,6},{5,7},{6,4},{7,5},{8,10},{9,11},{10,... | collective-permute-start | bytes 1572872 | tf_op jit(solution)/shard_map/cond/branch_2_fun/ppermute | solution.py:353
  128.5 29.2 %collective-permute-start.50 = (bf16[4,4,32,512]{3,2,1,0:T(8,128)(2,1)}, bf16[4,4,32,512]{3,2,1,0:T(8,128)(2,1)S(1)}, u32[]{:S(2)}, u32[]{:S(2)}) collective-permute-start(bf16[4,4,32,512]{3,2,1,0:T(8,128)(2,1)} %get-tuple-element.277), channel_id=1, source_target_pairs={{0,3},{1,0},{2,1},{3,2},{4,7},{5,4},{6,5},{7,6},{8,11},{9,8},{10,9... | collective-permute-start | bytes 1572872 | tf_op jit(solution)/shard_map/cond/branch_2_fun/ppermute | solution.py:353
  (7 other events, 57.4 us)

commit v3 on v2

--- a/solution.py
+++ b/solution.py
@@ -20,103 +20,100 @@
 SMALL = pl.CostEstimate(flops=0, bytes_accessed=1024, transcendentals=0)
 
 
-def lists_kernel(dims, caps, where, known, lists, places, pick, slot):
+def prepare_kernel(dims, caps, where, *rest):
     groups, planes, adapters, stride, own = dims
+    facts, panels = rest[:groups], rest[groups]
+    sent, (lists, places, pick, slot, known, sems) = rest[groups + 1 : groups + 1 + PLANE], rest[groups + 1 + PLANE :]
     plane_blocks = PLANE * own
     blocks = planes * plane_blocks
     row = blocks + planes * PLANE
-    my_plane, my_group = where[0], where[1]
-
-    def clear_slot(i, carry):
-        slot[i] = -1
-        return carry
-
-    def clear_list(i, carry):
-        lists[i] = 0
-        return carry
-
-    lax.fori_loop(0, planes * adapters, clear_slot, 0)
-    lax.fori_loop(0, planes * stride, clear_list, 0)
+    my_plane, my_group, my_shard = where[0], where[1], where[2]
+
+    for t, out in enumerate(sent):
+        shard = lax.rem(my_shard + t, PLANE)
+
+        def send(s, carry, out=out, shard=shard, t=t):
+            base = (lax.rem(my_plane + s, planes) * PLANE + shard) * own
+            for b in range(own):
+                pltpu.make_async_copy(panels.at[facts[0][base + b]], out.at[s, b], sems.at[t]).start()
+            return carry
+
+        lax.fori_loop(0, planes, send, 0)
+
+    for d, fact in enumerate(facts):
+        base = lax.rem(my_group - d + groups, groups) * row
+
+        def keep(i, carry, fact=fact, base=base):
+            for k in range(PLANE):
+                known[base + i * PLANE + k] = fact[i * PLANE + k]
+            return carry
+
+        lax.fori_loop(0, row // PLANE, keep, 0)
 
     def one_plane(plane, largest):
-        def one_group(group, found):
-            base = lax.rem(my_group - group + groups, groups) * row
-
-            def one_shard(shard, found):
-                count = known[base + blocks + plane * PLANE + shard]
+        at_slot, at_list = plane * adapters, plane * stride
+
+        def clear(i, carry):
+            for k in range(8):
+                slot[at_slot + i * 8 + k] = -1
+            return carry
+
+        lax.fori_loop(0, adapters // 8, clear, 0)
+        found = jnp.int32(0)
+        for group in range(groups):
+            for shard in range(PLANE):
+                count = known[group * row + blocks + plane * PLANE + shard]
                 for k in range(own):
-                    adapter = known[base + plane * plane_blocks + shard * own + k]
-                    at = plane * adapters + adapter
-                    held = slot[at]
+                    adapter = known[group * row + plane * plane_blocks + shard * own + k]
+                    held = slot[at_slot + adapter]
                     new = jnp.logical_and(count > k * BLOCK, held < 0)
-                    slot[at] = jnp.where(new, found, held)
-                    lists[plane * stride + found] = jnp.where(new, adapter, 0)
+                    slot[at_slot + adapter] = jnp.where(new, found, held)
+                    lists[at_list + found] = adapter
                     found = found + new.astype(jnp.int32)
-                return found
-
-            return lax.fori_loop(0, PLANE, one_shard, found)
-
-        return jnp.maximum(largest, lax.fori_loop(0, groups, one_group, 0))
-
-    largest = lax.fori_loop(0, planes, one_plane, 0)
+
+        def fill(i, carry):
+            lists[at_list + i] = 0
+            return carry
+
+        lax.fori_loop(found, stride, fill, 0)
+        return jnp.maximum(largest, found)
+
+    largest = lax.fori_loop(0, planes, one_plane, jnp.int32(0))
     branch = jnp.int32(0)
     for cap in caps[:-1]:
         branch = branch + (largest > cap).astype(jnp.int32)
     pick[0] = branch
 
-    def one_place(i, carry):
-        group, block = i // plane_blocks, lax.rem(i, plane_blocks)
-        base = lax.rem(my_group - group + groups, groups) * row
-        adapter = known[base + my_plane * plane_blocks + block]
-        places[i] = jnp.maximum(slot[my_plane * adapters + adapter], 0)
+    def one_group(group, carry):
+        for block in range(plane_blocks):
+            adapter = known[group * row + my_plane * plane_blocks + block]
+            places[group * plane_blocks + block] = jnp.maximum(slot[my_plane * adapters + adapter], 0)
         return carry
 
-    lax.fori_loop(0, groups * plane_blocks, one_place, 0)
-
-
-def make_lists(dims, caps, where, known):
+    lax.fori_loop(0, groups, one_group, 0)
+    for t, out in enumerate(sent):
+        pltpu.make_async_copy(out, out, sems.at[t]).wait()
+
+
+def prepare(dims, caps, where, facts, panels):
     groups, planes, adapters, stride, own = dims
     ints = lambda n: jax.ShapeDtypeStruct((n,), jnp.int32)
-    return pl.pallas_call(
-        functools.partial(lists_kernel, dims, caps),
-        out_shape=(ints(planes * stride), ints(groups * PLANE * own), ints(1)),
-        in_specs=[SMEM, SMEM],
-        out_specs=(SMEM, SMEM, SMEM),
-        scratch_shapes=[pltpu.SMEM((planes * adapters,), jnp.int32)],
-        name="lists",
-    )(where, known)
-
-
-def spread_kernel(planes, where, ids, panels, *rest):
-    outs, sems = rest[:-1], rest[-1]
-    own = outs[0].shape[1]
-    for t, out in enumerate(outs):
-        shard = lax.rem(where[2] + t, PLANE)
-
-        def send(s, carry, out=out, shard=shard, t=t):
-            base = (lax.rem(where[0] + s, planes) * PLANE + shard) * own
-            for b in range(own):
-                pltpu.make_async_copy(panels.at[ids[base + b]], out.at[s, b], sems.at[t]).start()
-            return carry
-
-        lax.fori_loop(0, planes, send, 0)
-    for t, out in enumerate(outs):
-        pltpu.make_async_copy(out, out, sems.at[t]).wait()
-
-
-def spread(dims, where, ids, panels):
-    groups, planes, adapters, stride, own = dims
-    out = jax.ShapeDtypeStruct((planes, own, *panels.shape[1:]), panels.dtype)
-    return pl.pallas_call(
-        functools.partial(spread_kernel, planes),
-        out_shape=(out,) * PLANE,
-        in_specs=[SMEM, SMEM, VMEM],
-        out_specs=(HBM,) * PLANE,
-        scratch_shapes=[pltpu.SemaphoreType.DMA((PLANE,))],
-        compiler_params=pltpu.CompilerParams(vmem_limit_bytes=VMEM_BYTES),
-        cost_estimate=SMALL,
-        name="spread",
-    )(where, ids, panels)
+    sent = jax.ShapeDtypeStruct((planes, own, *panels.shape[1:]), panels.dtype)
+    row = planes * PLANE * (own + 1)
+    return pl.pallas_call(
+        functools.partial(prepare_kernel, dims, caps),
+        out_shape=(*(sent,) * PLANE, ints(planes * stride), ints(groups * PLANE * own), ints(1)),
+        in_specs=[SMEM, *[SMEM] * groups, VMEM],
+        out_specs=(*(HBM,) * PLANE, SMEM, SMEM, SMEM),
+        scratch_shapes=[
+            pltpu.SMEM((planes * adapters,), jnp.int32),
+            pltpu.SMEM((groups * row,), jnp.int32),
+            pltpu.SemaphoreType.DMA((PLANE,)),
+        ],
+        compiler_params=pltpu.CompilerParams(vmem_limit_bytes=VMEM_BYTES),
+        cost_estimate=SMALL,
+        name="prepare",
+    )(where, *facts, panels)
 
 
 def regroup_kernel(planes, where, *refs):
@@ -327,7 +324,7 @@
     adapters = shrink_panels.shape[0]
     most = min(adapters, groups * PLANE * own)
     dims = (groups, planes, adapters, most + 1, own)
-    caps = tuple(most * part // 16 for part in (8, 9, 10, 11, 13, 16))
+    caps = tuple(most * part // 32 for part in (15, 16, 17, 18, 19, 20, 21, 23, 26, 32))
 
     ids = block_adapter.reshape(-1)
     me, group = lax.axis_index("blk"), lax.axis_index("groups")
@@ -336,7 +333,7 @@
     known = [facts]
     for d in range(1, groups):
         known.append(lax.ppermute(facts, "groups", [(i, (i + d) % groups) for i in range(groups)]))
-    lists, places, pick = make_lists(dims, caps, where, jnp.concatenate(known))
+    *up_sent, lists, places, pick = prepare(dims, caps, where, known, expand_panels)
     plane_ids = lax.dynamic_slice_in_dim(ids, me // PLANE * PLANE * own, PLANE * own, 0)
     mine = lax.dynamic_slice_in_dim(ids, me * own, own, 0)
     count = lax.dynamic_slice_in_dim(shard_counts, me, 1, 0)
@@ -356,7 +353,6 @@
     parts = 2 if rank % (2 * groups * ROWS) == 0 else 1
     ranks = rank // parts
 
-    up_sent = spread(dims, where, ids, expand_panels)
 
     def run(cap):
         def branch(up_sent):

time: 181 us -> 172 us (0.950); the launches traced: 183 us -> 170 us
  waiting for transfers between devices: 99.5 us -> 94 us
  Pallas kernels: 40.2 us -> 36 us
  starting transfers between devices: 36.5 us -> 34.5 us
    ppermute x6, waiting for transfers between devices: 33.7 us -> 19.6 us  [plane_shift(): lax.ppermute(x, 'blk', [(i, (i + s * PLANE) % devices) for i in range(dev...]
    ppermute x9, waiting for transfers between devices: 29.1 us -> 33.5 us  [shard_shift(): return lax.ppermute(x, 'blk', pairs)]
    pallas_call x2 -> x1, Pallas kernels: 9.64 us -> 5.85 us  [prepare(): pl.pallas_call(functools.partial(prepare_kernel, dims, caps), out_shape=(...]
  transfers between devices with their start and end apart: 19 -> 19, of which waited for: 12 -> 13; matrix products, arithmetic and copies ran while one was open for 1% -> 1% of each run, Pallas kernels for 16% -> 14%
where the time goes in v3:
time: 172 us; the launch traced here: 170 us
  waiting for transfers between devices  94 us (55%)
  Pallas kernels  36 us (21%)
  starting transfers between devices  34.5 us (20%)
  local copies, waits for them, and re-layouts  4.11 us (2%)
    ppermute x9, waiting for transfers between devices, shard_shift(): return lax.ppermute(x, 'blk', pairs)  33.5 us
    ppermute x2, waiting for transfers between devices, group_shift(): lax.ppermute(x, 'groups', [(i, (i + d) % groups) for i in range(groups)])  25.4 us
    ppermute x6, waiting for transfers between devices, plane_shift(): lax.ppermute(x, 'blk', [(i, (i + s * PLANE) % devices) for i in range(dev...  19.6 us
    all_to_all x1, waiting for transfers between devices, branch(): lax.all_to_all(up_packed, 'blk', split_axis=0, concat_axis=0, tiled=True,...  14.1 us
    ppermute x6, starting transfers between devices, plane_shift(): lax.ppermute(x, 'blk', [(i, (i + s * PLANE) % devices) for i in range(dev...  13.5 us
    ppermute x9, starting transfers between devices, shard_shift(): return lax.ppermute(x, 'blk', pairs)  9.98 us
    pallas_call x1, Pallas kernels, expand(): pl.pallas_call(functools.partial(expand_kernel, planes), grid=(own,), out...  6.22 us
    all_to_all x1, starting transfers between devices, branch(): lax.all_to_all(up_packed, 'blk', split_axis=0, concat_axis=0, tiled=True,...  5.93 us
  transfers between devices with their start and end apart: 19, of which 13 were waited for; matrix products, arithmetic and copies ran while one was open for 1% of the time, Pallas kernels for 14%

profile of v3, /device:TPU:0, one launch (start us, length us, event | category | flops | bytes accessed | tf_op | source)
XLA Modules:
  0.0 170.4 jit_solution(13317305058281049266)
XLA Ops:
  0.7 2.9 %collective-permute-start.170 = (s32[80]{0:T(128)S(1)}, s32[80]{0:T(128)S(1)}, u32[]{:S(2)}, u32[]{:S(2)}) collective-permute-start(s32[80]{0:T(128)S(1)} %pad_add_fusion.1.rest_0_), channel_id=1, source_target_pairs={{0,16},{16,0},{1,17},{17,1},{2,18},{18,2},{3,19},{19,3},{4,20},{20... | collective-permute-start | bytes 968 | tf_op jit(solution)/shard_map/ppermute | solution.py:335
  5.7 5.8 %prepare.1 = (bf16[4,4,64,512]{3,2,1,0:T(8,128)(2,1)S(1)}, bf16[4,4,64,512]{3,2,1,0:T(8,128)(2,1)}, bf16[4,4,64,512]{3,2,1,0:T(8,128)(2,1)}, bf16[4,4,64,512]{3,...) custom-call(s32[3]{0:T(128)S(1)} %pad_add_fusion.where, s32[80]{0:T(128)} %copy-done.104, ...), custom_call_target="tpu_custom_call" | custom-call | bytes 1024 | tf_op jit(solution)/shard_map/prepare/pallas_call | solution.py:103
  12.3 158.1 %conditional.1 = (bf16[256,8192]{1,0:T(8,128)(2,1)}) conditional(s32[]{:T(128)} %bitcast.24, (s32[3]{0:T(128)S(1)}, s32[132]{0:T(256)S(1)}, bf16[32,64,512]{2,1,0:T(8,128)(2,1)}, s32[32]{0:T(128)S(1)}, s32[64,1]{0,1:T(1,128)}, /*index=5*/bf16[4,4,64,512]{3,2,1,0:T(8,128)(2,1)}, bf16[4,4,64,512]{3,2,1,0:T(8,128)(2,1)}, ...), branch_computations={%region_0.1_spmd, %region_1.2_spmd, %region_2.3_spmd, %region_3.4_... | conditional | flops 8 | bytes 84947024 | solution.py:384
  15.9 2.6 %plane_pack.22 = (bf16[16,16,512]{2,1,0:T(8,128)(2,1)}, bf16[16,16,512]{2,1,0:T(8,128)(2,1)}, bf16[16,16,512]{2,1,0:T(8,128)(2,1)}) custom-call(s32[3]{0:T(128)S(1)} %get-tuple-element.313.where, s32[132]{0:T(256)S(1)} %get-tuple-element.321.lists, bf16[32,64,512]{2,1,0:T(8,128)(2,1)} %get-tuple-element.320.panels), custom_call_target="tpu_custom_call" | custom-call | bytes 1024 | tf_op jit(solution)/shard_map/cond/branch_1_fun/plane_pack/pallas_call | solution.py:161
  20.1 2.6 %collective-permute-start.18 = (bf16[16,16,512]{2,1,0:T(8,128)(2,1)}, bf16[16,16,512]{2,1,0:T(8,128)(2,1)S(1)}, u32[]{:S(2)}, u32[]{:S(2)}) collective-permute-start(bf16[16,16,512]{2,1,0:T(8,128)(2,1)} %get-tuple-element.323), channel_id=1, source_target_pairs={{0,8},{1,9},{2,10},{3,11},{4,12},{5,13},{6,14},{7,15},{8,0},{9,1},... | collective-permute-start | bytes 786440 | tf_op jit(solution)/shard_map/cond/branch_1_fun/ppermute | solution.py:343
  22.7 7.2 %collective-permute-done.17.rest_0_ = bf16[16,16,512]{2,1,0:T(8,128)(2,1)S(1)} collective-permute-done((bf16[16,16,512]{2,1,0:T(8,128)(2,1)}, bf16[16,16,512]{2,1,0:T(8,128)(2,1)S(1)}, u32[]{:S(2)}, u32[]{:S(2)}) %collective-permute-start.17) | collective-permute-done | bytes 262176 | tf_op jit(solution)/shard_map/cond/branch_1_fun/ppermute | solution.py:343
  30.3 2.6 %plane_pack.23 = (bf16[16,16,512]{2,1,0:T(8,128)(2,1)}, bf16[16,16,512]{2,1,0:T(8,128)(2,1)}, bf16[16,16,512]{2,1,0:T(8,128)(2,1)}) custom-call(s32[3]{0:T(128)S(1)} %get-tuple-element.313.where, s32[132]{0:T(256)S(1)} %get-tuple-element.321.lists, bf16[32,64,512]{2,1,0:T(8,128)(2,1)} %get-tuple-element.320.panels), custom_call_target="tpu_custom_call" | custom-call | bytes 1024 | tf_op jit(solution)/shard_map/cond/branch_1_fun/plane_pack/pallas_call | solution.py:161
  32.9 6.3 %collective-permute-done.18.rest_1_ = bf16[16,16,512]{2,1,0:T(8,128)(2,1)S(1)} collective-permute-done((bf16[16,16,512]{2,1,0:T(8,128)(2,1)}, bf16[16,16,512]{2,1,0:T(8,128)(2,1)S(1)}, u32[]{:S(2)}, u32[]{:S(2)}) %collective-permute-start.18) | collective-permute-done | bytes 262176 | tf_op jit(solution)/shard_map/cond/branch_1_fun/ppermute | solution.py:343
  39.3 5.3 %collective-permute-done.19.rest_2_ = bf16[16,16,512]{2,1,0:T(8,128)(2,1)S(1)} collective-permute-done((bf16[16,16,512]{2,1,0:T(8,128)(2,1)}, bf16[16,16,512]{2,1,0:T(8,128)(2,1)S(1)}, u32[]{:S(2)}, u32[]{:S(2)}) %collective-permute-start.19) | collective-permute-done | bytes 262176 | tf_op jit(solution)/shard_map/cond/branch_1_fun/ppermute | solution.py:343
  44.5 4.0 %collective-permute-start.24 = (bf16[16,16,512]{2,1,0:T(8,128)(2,1)}, bf16[16,16,512]{2,1,0:T(8,128)(2,1)}, u32[]{:S(2)}, u32[]{:S(2)}) collective-permute-start(bf16[16,16,512]{2,1,0:T(8,128)(2,1)} %get-tuple-element.335), channel_id=1, source_target_pairs={{0,4},{1,5},{2,6},{3,7},{4,8},{5,9},{6,10},{7,11},{8,12},{9,13},{1... | collective-permute-start | bytes 786440 | tf_op jit(solution)/shard_map/cond/branch_1_fun/ppermute | solution.py:343
  50.5 2.9 %collective-permute-start.26 = (bf16[16,16,512]{2,1,0:T(8,128)(2,1)}, bf16[16,16,512]{2,1,0:T(8,128)(2,1)}, u32[]{:S(2)}, u32[]{:S(2)}) collective-permute-start(bf16[16,16,512]{2,1,0:T(8,128)(2,1)} %get-tuple-element.337), channel_id=1, source_target_pairs={{0,12},{1,13},{2,14},{3,15},{4,0},{5,1},{6,2},{7,3},{8,4},{9,5},{1... | collective-permute-start | bytes 786440 | tf_op jit(solution)/shard_map/cond/branch_1_fun/ppermute | solution.py:343
  53.5 6.7 %collective-permute-done.29.refs_3_ = bf16[4,4,64,512]{3,2,1,0:T(8,128)(2,1)} collective-permute-done((bf16[4,4,64,512]{3,2,1,0:T(8,128)(2,1)}, bf16[4,4,64,512]{3,2,1,0:T(8,128)(2,1)}, u32[]{:S(2)}, u32[]{:S(2)}) %collective-permute-start.29) | collective-permute-done | bytes 1048608 | tf_op jit(solution)/shard_map/cond/branch_1_fun/ppermute | solution.py:350
  60.2 3.9 %regroup.11 = bf16[4,4,4,64,512]{4,3,2,1,0:T(8,128)(2,1)} custom-call(s32[3]{0:T(128)S(1)} %get-tuple-element.313.where, bf16[4,4,64,512]{3,2,1,0:T(8,128)(2,1)S(1)} %get-tuple-element.338.refs_0_, bf16[4,4,64,512]{3,2,1,0:T(8,128)(2,1)} %copy-done.37, bf16[4,4,64,512]{3,2,1,0:T(8,128)(2,1)} %copy-done.46, ...), custom_call_target="tpu_custom_call" | custom-call | bytes 1024 | tf_op jit(solution)/shard_map/cond/branch_1_fun/regroup/pallas_call | solution.py:130
  64.9 5.9 %all-to-all-start.1 = ((bf16[4,4,4,64,512]{4,3,2,1,0:T(8,128)(2,1)}), bf16[4,4,4,64,512]{4,3,2,1,0:T(8,128)(2,1)}, u32[]{:S(2)}, u32[]{:S(2)}) async-start(bf16[4,4,4,64,512]{4,3,2,1,0:T(8,128)(2,1)} %regroup.11), calls=%async_computation.1 | async-start | bytes 8388608 | tf_op jit(solution)/shard_map/cond/branch_1_fun/all_to_all | solution.py:375
  77.7 16.0 %collective-permute-done.20.rest_3_ = bf16[16,3,16,512]{3,2,1,0:T(8,128)(2,1)} collective-permute-done((bf16[16,3,16,512]{3,2,1,0:T(8,128)(2,1)}, bf16[16,3,16,512]{3,2,1,0:T(8,128)(2,1)}, u32[]{:S(2)}, u32[]{:S(2)}) %collective-permute-start.20) | collective-permute-done | bytes 786464 | tf_op jit(solution)/shard_map/cond/branch_1_fun/ppermute | solution.py:346
  93.7 2.7 %shard_pack.22 = (bf16[4,4,32,512]{3,2,1,0:T(8,128)(2,1)}, bf16[4,4,32,512]{3,2,1,0:T(8,128)(2,1)}, bf16[4,4,32,512]{3,2,1,0:T(8,128)(2,1)}, bf16[4,4,32,512]{3,2,1,0:T(8,128)(2,1)}) custom-call(s32[3]{0:T(128)S(1)} %get-tuple-element.313.where, s32[32]{0:T(128)S(1)} %get-tuple-element.318.places, s32[16]{0:T(128)} %fusion.3.ids, ...), custom_call_target="tpu_custom_call" | custom-call | bytes 1024 | tf_op jit(solution)/shard_map/cond/branch_1_fun/shard_pack/pallas_call | solution.py:239
  99.6 9.3 %collective-permute-done.30.rest_3_ = bf16[16,3,16,512]{3,2,1,0:T(8,128)(2,1)S(1)} collective-permute-done((bf16[16,3,16,512]{3,2,1,0:T(8,128)(2,1)}, bf16[16,3,16,512]{3,2,1,0:T(8,128)(2,1)S(1)}, u32[]{:S(2)}, u32[]{:S(2)}) %collective-permute-start.30) | collective-permute-done | bytes 786464 | tf_op jit(solution)/shard_map/cond/branch_1_fun/ppermute | solution.py:346
  109.8 2.8 %shard_pack.23 = (bf16[4,4,32,512]{3,2,1,0:T(8,128)(2,1)}, bf16[4,4,32,512]{3,2,1,0:T(8,128)(2,1)}, bf16[4,4,32,512]{3,2,1,0:T(8,128)(2,1)}, bf16[4,4,32,512]{3,2,1,0:T(8,128)(2,1)}) custom-call(s32[3]{0:T(128)S(1)} %get-tuple-element.313.where, s32[32]{0:T(128)S(1)} %get-tuple-element.318.places, s32[16]{0:T(128)} %fusion.3.ids, ...), custom_call_target="tpu_custom_call" | custom-call | bytes 1024 | tf_op jit(solution)/shard_map/cond/branch_1_fun/shard_pack/pallas_call | solution.py:239
  117.1 4.9 %collective-permute-done.23.rest_3_ = bf16[4,4,32,512]{3,2,1,0:T(8,128)(2,1)} collective-permute-done((bf16[4,4,32,512]{3,2,1,0:T(8,128)(2,1)}, bf16[4,4,32,512]{3,2,1,0:T(8,128)(2,1)}, u32[]{:S(2)}, u32[]{:S(2)}) %collective-permute-start.23) | collective-permute-done | bytes 524320 | tf_op jit(solution)/shard_map/cond/branch_1_fun/ppermute | solution.py:350
  122.0 10.8 %collective-permute-done.31.rest_5_ = bf16[4,4,32,512]{3,2,1,0:T(8,128)(2,1)S(1)} collective-permute-done((bf16[4,4,32,512]{3,2,1,0:T(8,128)(2,1)}, bf16[4,4,32,512]{3,2,1,0:T(8,128)(2,1)S(1)}, u32[]{:S(2)}, u32[]{:S(2)}) %collective-permute-start.31) | collective-permute-done | bytes 524320 | tf_op jit(solution)/shard_map/cond/branch_1_fun/ppermute | solution.py:350
  134.0 9.9 %collective-permute-done.33.rest_7_ = bf16[4,4,32,512]{3,2,1,0:T(8,128)(2,1)S(1)} collective-permute-done((bf16[4,4,32,512]{3,2,1,0:T(8,128)(2,1)}, bf16[4,4,32,512]{3,2,1,0:T(8,128)(2,1)S(1)}, u32[]{:S(2)}, u32[]{:S(2)}) %collective-permute-start.33) | collective-permute-done | bytes 524320 | tf_op jit(solution)/shard_map/cond/branch_1_fun/ppermute | solution.py:350
  144.7 5.4 %shrink.11.shrunk = bf16[256,64]{1,0:T(8,128)(2,1)} custom-call(s32[3]{0:T(128)S(1)} %get-tuple-element.313.where, bf16[256,8192]{1,0:T(8,128)(2,1)} %get-tuple-element.752.tokens, bf16[4,4,32,512]{3,2,1,0:T(8,128)(2,1)} %get-tuple-element.331.rest_0_, bf16[4,4,32,512]{3,2,1,0:T(8,128)(2,1)} %collective-permute-done.21.rest_1_, ...), custom_call_target="tpu_custom_call" | custom-call | bytes 1024 | tf_op jit(solution)/shard_map/cond/branch_1_fun/shrink/pallas_call | solution.py:271
  150.1 14.1 %all-to-all-done.1.maps = bf16[4,4,4,64,512]{4,3,2,1,0:T(8,128)(2,1)} async-done(((bf16[4,4,4,64,512]{4,3,2,1,0:T(8,128)(2,1)}), bf16[4,4,4,64,512]{4,3,2,1,0:T(8,128)(2,1)}, u32[]{:S(2)}, u32[]{:S(2)}) %all-to-all-start.1) | async-done | bytes 4194336 | tf_op jit(solution)/shard_map/cond/branch_1_fun/all_to_all | solution.py:375
  164.1 6.2 %expand.11 = bf16[256,8192]{1,0:T(8,128)(2,1)} custom-call(s32[3]{0:T(128)S(1)} %get-tuple-element.313.where, s32[4]{0:T(128)} %fusion.2.ids, s32[1]{0:T(128)} %dynamic_slice.39.count, f32[32]{0:T(128)S(1)} %copy-done.95, bf16[256,64]{1,0:T(8,128)(2,1)} %shrink.11.shrunk, bf16[4,4,4,64,512]{4,3,2,1,0:T(8,128)(2,1)} %all-to-all-done.1.maps), custom_call_target="tpu_custom_call" | custom-call | bytes 1024 | tf_op jit(solution)/shard_map/cond/branch_1_fun/expand/pallas_call | solution.py:304
  (60 shorter events, 28.6 us)
Async XLA Ops:
  0.7 4.5 %collective-permute-start.170 = (s32[80]{0:T(128)S(1)}, s32[80]{0:T(128)S(1)}, u32[]{:S(2)}, u32[]{:S(2)}) collective-permute-start(s32[80]{0:T(128)S(1)} %pad_add_fusion.1.rest_0_), channel_id=1, source_target_pairs={{0,16},{16,0},{1,17},{17,1},{2,18},{18,2},{3,19},{19,3},{4,20},{20... | collective-permute-start | bytes 968 | tf_op jit(solution)/shard_map/ppermute | solution.py:335
  12.3 38.2 %collective-permute-start.27 = (bf16[4,4,64,512]{3,2,1,0:T(8,128)(2,1)}, bf16[4,4,64,512]{3,2,1,0:T(8,128)(2,1)S(1)}, u32[]{:S(2)}, u32[]{:S(2)}) collective-permute-start(bf16[4,4,64,512]{3,2,1,0:T(8,128)(2,1)} %get-tuple-element.339), channel_id=1, source_target_pairs={{0,1},{1,2},{2,3},{3,0},{4,5},{5,6},{6,7},{7,4},{8,9},{9,10},{10,1... | collective-permute-start | bytes 3145736 | tf_op jit(solution)/shard_map/cond/branch_1_fun/ppermute | solution.py:350
  12.4 41.1 %collective-permute-start.28 = (bf16[4,4,64,512]{3,2,1,0:T(8,128)(2,1)}, bf16[4,4,64,512]{3,2,1,0:T(8,128)(2,1)S(1)}, u32[]{:S(2)}, u32[]{:S(2)}) collective-permute-start(bf16[4,4,64,512]{3,2,1,0:T(8,128)(2,1)} %get-tuple-element.340), channel_id=1, source_target_pairs={{0,2},{1,3},{2,0},{3,1},{4,6},{5,7},{6,4},{7,5},{8,10},{9,11},{10,... | collective-permute-start | bytes 3145736 | tf_op jit(solution)/shard_map/cond/branch_1_fun/ppermute | solution.py:350
  14.5 45.7 %collective-permute-start.29 = (bf16[4,4,64,512]{3,2,1,0:T(8,128)(2,1)}, bf16[4,4,64,512]{3,2,1,0:T(8,128)(2,1)}, u32[]{:S(2)}, u32[]{:S(2)}) collective-permute-start(bf16[4,4,64,512]{3,2,1,0:T(8,128)(2,1)} %get-tuple-element.341), channel_id=1, source_target_pairs={{0,3},{1,0},{2,1},{3,2},{4,7},{5,4},{6,5},{7,6},{8,11},{9,8},{10,9... | collective-permute-start | bytes 3145736 | tf_op jit(solution)/shard_map/cond/branch_1_fun/ppermute | solution.py:350
  18.5 11.4 %collective-permute-start.17 = (bf16[16,16,512]{2,1,0:T(8,128)(2,1)}, bf16[16,16,512]{2,1,0:T(8,128)(2,1)S(1)}, u32[]{:S(2)}, u32[]{:S(2)}) collective-permute-start(bf16[16,16,512]{2,1,0:T(8,128)(2,1)} %get-tuple-element.322), channel_id=1, source_target_pairs={{0,4},{1,5},{2,6},{3,7},{4,8},{5,9},{6,10},{7,11},{8,12},{9,13},{1... | collective-permute-start | bytes 786440 | tf_op jit(solution)/shard_map/cond/branch_1_fun/ppermute | solution.py:343
  20.1 19.2 %collective-permute-start.18 = (bf16[16,16,512]{2,1,0:T(8,128)(2,1)}, bf16[16,16,512]{2,1,0:T(8,128)(2,1)S(1)}, u32[]{:S(2)}, u32[]{:S(2)}) collective-permute-start(bf16[16,16,512]{2,1,0:T(8,128)(2,1)} %get-tuple-element.323), channel_id=1, source_target_pairs={{0,8},{1,9},{2,10},{3,11},{4,12},{5,13},{6,14},{7,15},{8,0},{9,1},... | collective-permute-start | bytes 786440 | tf_op jit(solution)/shard_map/cond/branch_1_fun/ppermute | solution.py:343
  29.9 34.2 %copy-start.48 = (bf16[16,16,512]{2,1,0:T(8,128)(2,1)}, bf16[16,16,512]{2,1,0:T(8,128)(2,1)S(1)}, u32[]{:S(2)}) copy-start(bf16[16,16,512]{2,1,0:T(8,128)(2,1)S(1)} %collective-permute-done.17.rest_0_) | copy-start | bytes 786436 | tf_op jit(solution)/shard_map/cond
  29.9 14.7 %collective-permute-start.19 = (bf16[16,16,512]{2,1,0:T(8,128)(2,1)}, bf16[16,16,512]{2,1,0:T(8,128)(2,1)S(1)}, u32[]{:S(2)}, u32[]{:S(2)}) collective-permute-start(bf16[16,16,512]{2,1,0:T(8,128)(2,1)} %get-tuple-element.324), channel_id=1, source_target_pairs={{0,12},{1,13},{2,14},{3,15},{4,0},{5,1},{6,2},{7,3},{8,4},{9,5},{1... | collective-permute-start | bytes 786440 | tf_op jit(solution)/shard_map/cond/branch_1_fun/ppermute | solution.py:343
  39.2 20.9 %copy-start.49 = (bf16[16,16,512]{2,1,0:T(8,128)(2,1)}, bf16[16,16,512]{2,1,0:T(8,128)(2,1)S(1)}, u32[]{:S(2)}) copy-start(bf16[16,16,512]{2,1,0:T(8,128)(2,1)S(1)} %collective-permute-done.18.rest_1_) | copy-start | bytes 786436 | tf_op jit(solution)/shard_map/cond
  44.5 19.5 %collective-permute-start.24 = (bf16[16,16,512]{2,1,0:T(8,128)(2,1)}, bf16[16,16,512]{2,1,0:T(8,128)(2,1)}, u32[]{:S(2)}, u32[]{:S(2)}) collective-permute-start(bf16[16,16,512]{2,1,0:T(8,128)(2,1)} %get-tuple-element.335), channel_id=1, source_target_pairs={{0,4},{1,5},{2,6},{3,7},{4,8},{5,9},{6,10},{7,11},{8,12},{9,13},{1... | collective-permute-start | bytes 786440 | tf_op jit(solution)/shard_map/cond/branch_1_fun/ppermute | solution.py:343
  48.5 16.4 %collective-permute-start.25 = (bf16[16,16,512]{2,1,0:T(8,128)(2,1)}, bf16[16,16,512]{2,1,0:T(8,128)(2,1)}, u32[]{:S(2)}, u32[]{:S(2)}) collective-permute-start(bf16[16,16,512]{2,1,0:T(8,128)(2,1)} %get-tuple-element.336), channel_id=1, source_target_pairs={{0,8},{1,9},{2,10},{3,11},{4,12},{5,13},{6,14},{7,15},{8,0},{9,1},... | collective-permute-start | bytes 786440 | tf_op jit(solution)/shard_map/cond/branch_1_fun/ppermute | solution.py:343
  50.5 14.4 %collective-permute-start.26 = (bf16[16,16,512]{2,1,0:T(8,128)(2,1)}, bf16[16,16,512]{2,1,0:T(8,128)(2,1)}, u32[]{:S(2)}, u32[]{:S(2)}) collective-permute-start(bf16[16,16,512]{2,1,0:T(8,128)(2,1)} %get-tuple-element.337), channel_id=1, source_target_pairs={{0,12},{1,13},{2,14},{3,15},{4,0},{5,1},{6,2},{7,3},{8,4},{9,5},{1... | collective-permute-start | bytes 786440 | tf_op jit(solution)/shard_map/cond/branch_1_fun/ppermute | solution.py:343
  64.1 29.6 %copy-start.1 = (bf16[32,64,512]{2,1,0:T(8,128)(2,1)S(1)}, bf16[32,64,512]{2,1,0:T(8,128)(2,1)}, u32[]{:S(2)}) copy-start(bf16[32,64,512]{2,1,0:T(8,128)(2,1)} %get-tuple-element.320.panels) | copy-start | bytes 6291460 | tf_op jit(solution)/shard_map/cond
  64.9 99.3 %all-to-all-start.1 = ((bf16[4,4,4,64,512]{4,3,2,1,0:T(8,128)(2,1)}), bf16[4,4,4,64,512]{4,3,2,1,0:T(8,128)(2,1)}, u32[]{:S(2)}, u32[]{:S(2)}) async-start(bf16[4,4,4,64,512]{4,3,2,1,0:T(8,128)(2,1)} %regroup.11), calls=%async_computation.1 | async-start | bytes 8388608 | tf_op jit(solution)/shard_map/cond/branch_1_fun/all_to_all | solution.py:375
  72.8 43.0 %copy-start.107 = (s32[16]{0:T(128)S(1)}, s32[16]{0:T(128)}, u32[]{:S(2)}) copy-start(s32[16]{0:T(128)} %get-tuple-element.693) | copy-start | bytes 196 | tf_op jit(solution)/shard_map/cond
  72.8 20.9 %collective-permute-start.20 = (bf16[16,3,16,512]{3,2,1,0:T(8,128)(2,1)}, bf16[16,3,16,512]{3,2,1,0:T(8,128)(2,1)}, u32[]{:S(2)}, u32[]{:S(2)}) collective-permute-start(bf16[16,3,16,512]{3,2,1,0:T(8,128)(2,1)} %group_pack.22), channel_id=1, source_target_pairs={{0,16},{16,0},{1,17},{17,1},{2,18},{18,2},{3,19},{19,3},{4,20},{20... | collective-permute-start | bytes 2359304 | tf_op jit(solution)/shard_map/cond/branch_1_fun/ppermute | solution.py:346
  76.4 32.5 %collective-permute-start.30 = (bf16[16,3,16,512]{3,2,1,0:T(8,128)(2,1)}, bf16[16,3,16,512]{3,2,1,0:T(8,128)(2,1)S(1)}, u32[]{:S(2)}, u32[]{:S(2)}) collective-permute-start(bf16[16,3,16,512]{3,2,1,0:T(8,128)(2,1)} %group_pack.23), channel_id=1, source_target_pairs={{0,16},{16,0},{1,17},{17,1},{2,18},{18,2},{3,19},{19,3},{4,20},{20... | collective-permute-start | bytes 2359304 | tf_op jit(solution)/shard_map/cond/branch_1_fun/ppermute | solution.py:346
  96.5 18.0 %collective-permute-start.21 = (bf16[4,4,32,512]{3,2,1,0:T(8,128)(2,1)}, bf16[4,4,32,512]{3,2,1,0:T(8,128)(2,1)}, u32[]{:S(2)}, u32[]{:S(2)}) collective-permute-start(bf16[4,4,32,512]{3,2,1,0:T(8,128)(2,1)} %get-tuple-element.332), channel_id=1, source_target_pairs={{0,1},{1,2},{2,3},{3,0},{4,5},{5,6},{6,7},{7,4},{8,9},{9,10},{10,1... | collective-permute-start | bytes 1572872 | tf_op jit(solution)/shard_map/cond/branch_1_fun/ppermute | solution.py:350
  96.5 20.6 %collective-permute-start.22 = (bf16[4,4,32,512]{3,2,1,0:T(8,128)(2,1)}, bf16[4,4,32,512]{3,2,1,0:T(8,128)(2,1)}, u32[]{:S(2)}, u32[]{:S(2)}) collective-permute-start(bf16[4,4,32,512]{3,2,1,0:T(8,128)(2,1)} %get-tuple-element.333), channel_id=1, source_target_pairs={{0,2},{1,3},{2,0},{3,1},{4,6},{5,7},{6,4},{7,5},{8,10},{9,11},{10,... | collective-permute-start | bytes 1572872 | tf_op jit(solution)/shard_map/cond/branch_1_fun/ppermute | solution.py:350
  98.2 23.8 %collective-permute-start.23 = (bf16[4,4,32,512]{3,2,1,0:T(8,128)(2,1)}, bf16[4,4,32,512]{3,2,1,0:T(8,128)(2,1)}, u32[]{:S(2)}, u32[]{:S(2)}) collective-permute-start(bf16[4,4,32,512]{3,2,1,0:T(8,128)(2,1)} %get-tuple-element.334), channel_id=1, source_target_pairs={{0,3},{1,0},{2,1},{3,2},{4,7},{5,4},{6,5},{7,6},{8,11},{9,8},{10,9... | collective-permute-start | bytes 1572872 | tf_op jit(solution)/shard_map/cond/branch_1_fun/ppermute | solution.py:350
  112.6 20.2 %collective-permute-start.31 = (bf16[4,4,32,512]{3,2,1,0:T(8,128)(2,1)}, bf16[4,4,32,512]{3,2,1,0:T(8,128)(2,1)S(1)}, u32[]{:S(2)}, u32[]{:S(2)}) collective-permute-start(bf16[4,4,32,512]{3,2,1,0:T(8,128)(2,1)} %get-tuple-element.346), channel_id=1, source_target_pairs={{0,1},{1,2},{2,3},{3,0},{4,5},{5,6},{6,7},{7,4},{8,9},{9,10},{10,1... | collective-permute-start | bytes 1572872 | tf_op jit(solution)/shard_map/cond/branch_1_fun/ppermute | solution.py:350
  112.6 21.4 %collective-permute-start.32 = (bf16[4,4,32,512]{3,2,1,0:T(8,128)(2,1)}, bf16[4,4,32,512]{3,2,1,0:T(8,128)(2,1)S(1)}, u32[]{:S(2)}, u32[]{:S(2)}) collective-permute-start(bf16[4,4,32,512]{3,2,1,0:T(8,128)(2,1)} %get-tuple-element.347), channel_id=1, source_target_pairs={{0,2},{1,3},{2,0},{3,1},{4,6},{5,7},{6,4},{7,5},{8,10},{9,11},{10,... | collective-permute-start | bytes 1572872 | tf_op jit(solution)/shard_map/cond/branch_1_fun/ppermute | solution.py:350
  114.5 29.4 %collective-permute-start.33 = (bf16[4,4,32,512]{3,2,1,0:T(8,128)(2,1)}, bf16[4,4,32,512]{3,2,1,0:T(8,128)(2,1)S(1)}, u32[]{:S(2)}, u32[]{:S(2)}) collective-permute-start(bf16[4,4,32,512]{3,2,1,0:T(8,128)(2,1)} %get-tuple-element.348), channel_id=1, source_target_pairs={{0,3},{1,0},{2,1},{3,2},{4,7},{5,4},{6,5},{7,6},{8,11},{9,8},{10,9... | collective-permute-start | bytes 1572872 | tf_op jit(solution)/shard_map/cond/branch_1_fun/ppermute | solution.py:350
  144.7 19.5 %copy-start.95 = (f32[32]{0:T(128)S(1)}, f32[32]{0:T(128)}, u32[]{:S(2)}) copy-start(f32[32]{0:T(128)} %get-tuple-element.822.scales) | copy-start | bytes 388 | tf_op jit(solution)/shard_map/cond
  (10 other events, 72.6 us)
